TPU v7x, 512 devices: a whole 4x4x16 slice. The times are simulated.
512 devices in a mesh: row: 16 (over z_lo, core), col: 32 (over y, x, z_hi).
Axes of the slice: x: 4, y: 4, z: 16 (z_hi: 2, z_lo: 8; z = z_hi * 8 + z_lo), core: 2. Of those that a mesh axis runs over, the one named last changes fastest.
Arguments:
- signatures: bfloat16 [8192, 49152], P('row', 'col'), as said below
- trailing: float32 [8192, 4096], P('row', 'col'), may hold values from -6 to 6
- ridge: float32 [1], replicated, may hold values from 0.5 to 2
- panel_index: int32 [1], replicated, may hold values from 1 to 15
Outputs:
- factor: float32 [8192, 256], P(('row', 'col'))
- updated: float32 [8192, 4096], P('row', 'col')
Inputs may be any that keep to these rules, and one draw needn't show every extreme that they name: `signatures`: every diagonal block of the Gram matrix plus the ridge is positive definite.
All inputs are finite; a program needn't handle non-finite values.
Results may differ from a plain program's by a relative error of at most 0.0003.
Values may be sent and summed in bfloat16 or wider, within the bound.
No kernel may reach another device: no remote copies, remote signals or barrier semaphores. Data moves between devices by JAX's collectives and lax.ppermute only.
A program may use at most 64 MiB of HBM per device.

v0:
```python
import jax
import jax.numpy as jnp
from jax import lax
from jax.sharding import PartitionSpec as P

PANEL = 256


def spread(block, axis, owner):
    block = jnp.where(lax.axis_index(axis) == owner, block, jnp.zeros_like(block))
    return lax.psum(block, axis)


def add_ridge(block, first_row, panel_start, ridge):
    row_ids = first_row + lax.broadcasted_iota(jnp.int32, block.shape, 0)
    col_ids = panel_start + lax.broadcasted_iota(jnp.int32, block.shape, 1)
    return block + jnp.where(row_ids == col_ids, ridge[0], jnp.zeros((), block.dtype))


def mask_above(block, first_row, panel_start):
    row_ids = first_row + lax.broadcasted_iota(jnp.int32, block.shape, 0)
    return jnp.where(row_ids >= panel_start, block, jnp.zeros((), block.dtype))


def solve_rows(lower, panel_rows):
    return jax.scipy.linalg.solve_triangular(lower, panel_rows.T, lower=True).T


def local(signatures, trailing, ridge, panel_index):
    rows_dev = signatures.shape[0]
    tile_cols = trailing.shape[1]
    col_count = lax.axis_size("col")
    row_share = rows_dev // col_count
    row_pos = lax.axis_index("row")
    col_pos = lax.axis_index("col")
    panel_start = panel_index[0] * PANEL
    row_owner = panel_start // rows_dev
    local_offset = panel_start % rows_dev
    own_paths = lax.dynamic_slice_in_dim(signatures, local_offset, PANEL, 0)
    panel_paths = spread(own_paths, "row", row_owner)
    mine_rows = lax.psum_scatter(
        lax.dot_general(
            signatures, panel_paths, (((1,), (1,)), ((), ())), preferred_element_type=jnp.float32
        ),
        "col",
        scatter_dimension=0,
        tiled=True,
    )
    mine_rows = add_ridge(mine_rows, row_pos * rows_dev + col_pos * row_share, panel_start, ridge)
    source_rows = lax.all_gather(mine_rows, "col", axis=0, tiled=True)
    block_cut = lax.dynamic_slice_in_dim(source_rows, local_offset, PANEL, 0)
    diagonal = spread(block_cut, "row", row_owner)
    lower = jnp.linalg.cholesky(diagonal)
    factor_mine = solve_rows(lower, mine_rows)
    factor_mine = mask_above(factor_mine, row_pos * rows_dev + col_pos * row_share, panel_start)
    factor_block = lax.all_gather(factor_mine, "col", axis=0, tiled=True)
    window_start = panel_start + PANEL + col_pos * tile_cols
    window_owner = window_start // rows_dev
    window_cut = lax.dynamic_slice_in_dim(factor_block, window_start % rows_dev, tile_cols, 0)
    window_rows = spread(window_cut, "row", window_owner)
    updated = trailing - lax.dot_general(
        factor_block,
        window_rows,
        (((1,), (1,)), ((), ())),
        precision=lax.Precision.HIGHEST,
        preferred_element_type=jnp.float32,
    )
    return (factor_mine, updated)


def solution(mesh):
    placed = (P("row", "col"), P("row", "col"), P(), P())
    return jax.shard_map(
        local,
        mesh=mesh,
        in_specs=placed,
        out_specs=(P(("row", "col"), None), P("row", "col")),
        check_vma=False,
    )
```

profile of v0, /device:TPU:1, one launch (start us, length us, event | category | flops | bytes accessed | tf_op | source)
XLA Modules:
  0.0 1291.1 jit_solution(10216238595232170383)
XLA Ops:
  8.0 2.3 dynamic-slice_select_fusion
  10.4 204.1 %all-reduce.5.cloned.1.call-done = bf16[256,1536]{1,0:T(8,128)(2,1)} async-done(((bf16[256,1536]{1,0:T(8,128)(2,1)}), bf16[256,1536]{1,0:T(8,128)(2,1)}) %all-reduce.5.cloned.1.call-update) | async-done | bytes 786448 | tf_op jit(solution)/shard_map/psum | solution.py:11
  214.4 1.7 convolution_bitcast_fusion
  216.2 1.0 copy.18
  217.9 283.6 %reduce-scatter.4.cloned.1.call-done = f32[16,256]{1,0:T(8,128)} async-done(((f32[512,256]{1,0:T(8,128)}), f32[16,256]{1,0:T(8,128)}) %reduce-scatter.4.cloned.1.call-update) | async-done | bytes 16400
  501.6 0.8 copy.19
  502.4 0.1 select_add_fusion
  502.5 137.0 %all_gather.6 = f32[512,256]{1,0:T(8,128)S(1)} all-gather(f32[16,256]{1,0:T(8,128)S(1)} %copy.11), channel_id=1, replica_groups=mesh['row'=16,'col'=32] {'col'}, dimensions={0}, use_global_device_ids=true | all-gather | bytes 540672 | tf_op jit(solution)/shard_map/all_gather | solution.py:50
  639.6 0.1 copy.21
  639.7 0.7 broadcast_select_fusion
  640.7 231.9 %all-reduce.7.cloned.1.call-done = f32[256,256]{0,1:T(8,128)} async-done(((f32[256,256]{0,1:T(8,128)}), f32[256,256]{0,1:T(8,128)}) %all-reduce.7.cloned.1.call-update) | async-done | bytes 262160 | tf_op jit(solution)/shard_map/psum | solution.py:11
  872.6 1.1 copy.13
  873.7 1.0 fusion
  874.7 11.7 cholesky.49
  886.4 9.8 custom-call.15
  896.3 0.2 fusion.5
  896.5 0.3 convolution_subtract_fusion.2
  896.7 11.7 cholesky.103
  908.8 0.6 compare_reduce_fusion
  910.9 4.4 while.1
  911.1 0.6 fusion.20
  911.6 1.4 dynamic-slice.7
  913.2 0.6 fusion.20
  913.8 1.4 dynamic-slice.7
  915.3 19.7 %custom-call.16 = f32[2,128,128]{1,2,0:T(8,128)S(1)} custom-call(f32[2,128,128]{2,1,0:T(8,128)S(1)} %get-tuple-element.9), custom_call_target="InvertDiagBlocksLowerTriangular" | custom-call | tf_op jit(solution)/shard_map/jit(_solve_triangular)/triangular_solve | solution.py:26
  935.0 0.2 fusion.3
  935.2 0.3 convolution_subtract_fusion.1
  935.5 0.2 fusion.2
  935.8 145.4 %all_gather.7 = f32[512,256]{1,0:T(8,128)S(1)} all-gather(f32[16,256]{1,0:T(8,128)S(1)} %fusion.8), channel_id=1, replica_groups=mesh['row'=16,'col'=32] {'col'}, dimensions={0}, use_global_device_ids=true | all-gather | bytes 540672 | tf_op jit(solution)/shard_map/all_gather | solution.py:56
  1081.2 0.7 dynamic-slice_select_fusion.1
  1081.9 200.4 %all-reduce.9.cloned.1.call-done = f32[128,256]{1,0:T(8,128)} async-done(((f32[128,256]{1,0:T(8,128)}), f32[128,256]{1,0:T(8,128)}) %all-reduce.9.cloned.1.call-update) | async-done | bytes 131088 | tf_op jit(solution)/shard_map/psum | solution.py:11
  1282.4 2.2 convolution_subtract_fusion
  (40 shorter events, 1.2 us)
Async XLA Ops:
  7.2 207.3 %copy-start = (bf16[512,1536]{1,0:T(8,128)(2,1)S(1)}, bf16[512,1536]{1,0:T(8,128)(2,1)}, u32[]{:S(2)}) copy-start(bf16[512,1536]{1,0:T(8,128)(2,1)} %param.4) | copy-start | bytes 4718596
  7.2 207.3 %all-reduce.5.cloned.1.call-start = ((), (), s32[]{:S(2)}) async-start(), calls=%async_computation.1 | async-start | bytes 1572864 | tf_op jit(solution)/shard_map/psum | solution.py:11
  10.3 491.2 %reduce-scatter.4.cloned.1.call-start = ((), (), s32[]{:S(2)}) async-start(), calls=%async_computation.4 | async-start | bytes 540672
  217.2 655.4 %all-reduce.7.cloned.1.call-start = ((), (), s32[]{:S(2)}) async-start(), calls=%async_computation.2 | async-start | bytes 524288 | tf_op jit(solution)/shard_map/psum | solution.py:11
  640.5 641.9 %all-reduce.9.cloned.1.call-start = ((), (), s32[]{:S(2)}) async-start(), calls=%async_computation.3 | async-start | bytes 262144 | tf_op jit(solution)/shard_map/psum | solution.py:11
  910.9 371.5 %copy-start.1 = (f32[512,128]{1,0:T(8,128)S(1)}, f32[512,128]{1,0:T(8,128)}, u32[]{:S(2)}) copy-start(f32[512,128]{1,0:T(8,128)} %param.5) | copy-start | bytes 786436
  935.8 348.7 %copy-start.2 = (f32[16,256]{1,0:T(8,128)}, f32[16,256]{1,0:T(8,128)S(1)}, u32[]{:S(2)}) copy-start(f32[16,256]{1,0:T(8,128)S(1)} %fusion.8) | copy-start | bytes 49156
Sparse Core Ops, SparseCore 0:
  10.9 203.4 all-reduce.4
  217.5 284.0 reduce-scatter.3
  640.6 231.9 all-reduce.6
  1082.0 200.2 all-reduce.8
where the time goes:
time: 1290 us
  waiting for transfers between devices  920 us (71%)
  blocking collectives  282 us (22%)
  other arithmetic  58.6 us (5%)
  between operations  16.8 us (1%)
    psum x3, waiting for transfers between devices, spread(): return lax.psum(block, axis)  636 us
    unnamed x5, waiting for transfers between devices  284 us
    all_gather x1, blocking collectives, local(): factor_block = lax.all_gather(factor_mine, 'col', axis=0, tiled=True)  145 us
    all_gather x1, blocking collectives, local(): source_rows = lax.all_gather(mine_rows, 'col', axis=0, tiled=True)  137 us
    another operation x6, other arithmetic, local(): lower = jnp.linalg.cholesky(diagonal)  34 us
  transfers between devices with their start and end apart: 4, of which 4 were waited for; matrix products, arithmetic and copies ran while one was open for 0% of the time, Pallas kernels for 0%

commit v1 on v0

v1 whole, which is shorter than its diff:
```python
import jax
import jax.numpy as jnp
from jax import lax
from jax.experimental import pallas as pl
from jax.experimental.pallas import tpu as pltpu
from jax.sharding import Mesh, PartitionSpec as P

PANEL = 256
HALF = 128
ROWS = 16
ROW = ("zl", "core")
PLANE = ("y", "x")
COL = ("y", "x", "zh")
HIGHEST = lax.Precision.HIGHEST
SWAP = [(0, 1), (1, 0)]
F32 = jnp.float32


def member(ids, position):
    bits = sum(1 << i for i in ids)
    return (jnp.int32(bits) >> position) & 1 == 1


def panel_tree(owner):
    def branch(own):
        row = lax.axis_index(ROW)
        held, block = [owner], own
        for step in (8, 4, 2):
            pairs = [(h, h + step) for h in held if h + step < ROWS]
            moved = lax.ppermute(block, ROW, pairs)
            block = jnp.where(member([t for _, t in pairs], row), moved, block)
            held = held + [t for _, t in pairs]
        return block

    return branch


def mm(a, b, ca, cb):
    return lax.dot_general(a, b, (((ca,), (cb,)), ((), ())), precision=HIGHEST, preferred_element_type=F32)


def call(kernel, outs, *args, flops=10**9):
    cost = pl.CostEstimate(flops=flops, bytes_accessed=10**6, transcendentals=0)
    vmem = pl.BlockSpec(memory_space=pltpu.VMEM)
    return pl.pallas_call(
        kernel,
        out_shape=outs,
        in_specs=[vmem] * len(args),
        out_specs=(vmem,) * len(outs) if isinstance(outs, tuple) else vmem,
        cost_estimate=cost,
    )(*args)


def gram_kernel(flag_ref, s_ref, own_ref, moved_ref, out_ref):
    panel = jnp.where(flag_ref[...] > 0, own_ref[...], moved_ref[...])
    dims = (((1,), (1,)), ((), ()))
    gram = lax.dot_general(s_ref[...], panel, dims, preferred_element_type=F32)
    diag = lax.dot_general(panel, panel, dims, preferred_element_type=F32)
    for k in range(16):
        out_ref[k, :32, :] = gram[32 * k : 32 * k + 32]
        out_ref[k, 32:, :] = diag[16 * k : 16 * k + 16]


def rsqrt(v):
    r = lax.rsqrt(v)
    return r * (1.5 - 0.5 * v * r * r)


def fill(v):
    return jnp.broadcast_to(v, (8, HALF))


GROUPS = HALF // 8


def eliminate(a, e, out_ref, first, last):
    sub = lax.broadcasted_iota(jnp.int32, (8, HALF), 0)
    for g in range(first, last):
        rows_a, rows_e = a[g], e[g]
        columns = [fill(rows_a[:, 8 * g + j : 8 * g + j + 1]) for j in range(8)]
        for s in range(8):
            pivot = fill(columns[s][s : s + 1])
            scale = 1.0 / pivot
            row_a, row_e = fill(rows_a[s : s + 1]), fill(rows_e[s : s + 1])
            k = 8 * g + s
            out_ref[k : k + 1, :] = (row_e * rsqrt(pivot))[:1]
            weight = jnp.where(sub == s, 1.0 - scale, columns[s] * scale)
            rows_a = rows_a - weight * row_a
            rows_e = rows_e - weight * row_e
            for j in range(s + 1, 8):
                columns[j] = columns[j] - weight * fill(columns[j][s : s + 1])
        solved_a = [fill(rows_a[t : t + 1]) for t in range(8)]
        solved_e = [fill(rows_e[t : t + 1]) for t in range(8)]
        for h in range(g + 1, GROUPS):
            below = [fill(a[h][:, 8 * g + t : 8 * g + t + 1]) for t in range(8)]
            a[h] = a[h] - sum(below[t] * solved_a[t] for t in range(8))
            e[h] = e[h] - sum(below[t] * solved_e[t] for t in range(8))


def split(v):
    return [v[8 * g : 8 * g + 8] for g in range(GROUPS)]


def start_block(d_ref, after_ref, a_ref, e_ref, m_ref):
    sub = lax.broadcasted_iota(jnp.int32, (8, HALF), 0)
    lane = lax.broadcasted_iota(jnp.int32, (8, HALF), 1)
    a, e = split(d_ref[...]), [jnp.where(lane == sub + 8 * g, 1.0, 0.0) for g in range(GROUPS)]
    eliminate(a, e, m_ref, 0, GROUPS // 2)
    for g in range(GROUPS // 2, GROUPS):
        a_ref[8 * g : 8 * g + 8, :] = a[g]
        e_ref[8 * g : 8 * g + 8, :] = e[g]


def end_block(a_ref, e_ref, m_in, m_ref):
    m_ref[: HALF // 2, :] = m_in[: HALF // 2, :]
    eliminate(split(a_ref[...]), split(e_ref[...]), m_ref, GROUPS // 2, GROUPS)
    return m_ref[...]


def end_upper(a_ref, e_ref, m_in, d10_ref, d11_ref, after_ref, m_ref, x_ref, d_ref):
    m = end_block(a_ref, e_ref, m_in, m_ref)
    low = mm(d10_ref[...], m, 1, 1)
    d_ref[...] = d11_ref[...] - mm(low, low, 1, 1)
    x_ref[...] = mm(low, m, 1, 0)


def end_lower(a_ref, e_ref, m_in, m00_ref, x_ref, after_ref, out_ref, m_ref):
    m = end_block(a_ref, e_ref, m_in, m_ref)
    out_ref[:HALF, :HALF] = m00_ref[...]
    out_ref[:HALF, HALF:] = jnp.zeros((HALF, HALF), F32)
    out_ref[HALF:, HALF:] = m
    out_ref[HALF:, :HALF] = -mm(m, x_ref[...], 1, 0)


SQUARE = jax.ShapeDtypeStruct((HALF, HALF), F32)
FULL = jax.ShapeDtypeStruct((PANEL, PANEL), F32)


def window_and_inverse(cut, source, diag):
    zl, core = lax.axis_index("zl"), lax.axis_index("core")
    rows = cut.shape[0] // 2
    halves = cut.reshape(2, rows, PANEL)
    mine = jnp.where(core == 0, halves[0], halves[1])
    other = jnp.where(core == 0, halves[1], halves[0])

    def cross(block, step):
        moved = lax.ppermute(block, "zl", [(i, i ^ step) for i in range(8)])
        return jnp.where((zl ^ (source >> 1)) & step != 0, moved, block)

    token = lambda v: v[:8, :HALF]
    block = jnp.where(core == (source & 1), mine, lax.ppermute(other, "core", SWAP))
    a, e, m = call(start_block, (SQUARE,) * 3, diag[:HALF, :HALF], token(diag))
    far = cross(block, 4)
    m00, x, d11 = call(end_upper, (SQUARE,) * 3, a, e, m, diag[HALF:, :HALF], diag[HALF:, HALF:], token(block))
    mid = cross(far, 2)
    a, e, m = call(start_block, (SQUARE,) * 3, d11, token(far))
    near = cross(mid, 1)
    inverse = call(end_lower, (FULL, SQUARE), a, e, m, m00, x, token(mid))[0]
    moved = lax.ppermute(near, "core", SWAP)
    return jnp.where(core == 0, jnp.concatenate([near, moved]), jnp.concatenate([moved, near])), inverse


def local(signatures, trailing, ridge, panel_index):
    rows_dev, tile_cols = signatures.shape[0], trailing.shape[1]
    row, col = lax.axis_index(ROW), lax.axis_index(COL)
    core = lax.axis_index("core")
    x, y, zh = lax.axis_index("x"), lax.axis_index("y"), lax.axis_index("zh")
    index = panel_index[0]
    panel_start = index * PANEL
    owner = index >> 1
    own = lax.dynamic_slice_in_dim(signatures, panel_start & (rows_dev - 1), PANEL, 0)
    panel = lax.switch(owner, [panel_tree(o) for o in range(8)], own)
    moved = lax.ppermute(panel, "core", SWAP)
    flag = jnp.full((1, 1), core == (owner & 1), jnp.int32)
    parts = call(gram_kernel, jax.ShapeDtypeStruct((16, 48, PANEL), F32), flag, signatures, panel, moved)
    parts = lax.all_to_all(parts, PLANE, 0, 0, tiled=True)
    piece = jnp.sum(parts, axis=0)
    piece = piece + lax.ppermute(piece, "zh", SWAP)
    pieces = lax.all_to_all(jnp.broadcast_to(piece[None], parts.shape), PLANE, 0, 0, tiled=True)

    cut_start = 8 * ((index + 1 + x) & 1) + 4 * zh
    cut = lax.dynamic_slice_in_dim(pieces, cut_start, 4, 0)[:, :32].reshape(tile_cols, PANEL)
    diag = pieces[:, 32:].reshape(PANEL, PANEL)
    eye = jnp.eye(PANEL, dtype=F32)
    diag = jnp.where(row >= owner, diag + ridge[0] * eye, eye)
    cut, inverse = window_and_inverse(cut, 2 * y + ((index + 1 + x) >> 1), diag)

    gram = pieces[:, :32].reshape(rows_dev, PANEL)
    row_ids = row * rows_dev + lax.broadcasted_iota(jnp.int32, gram.shape, 0)
    col_ids = panel_start + lax.broadcasted_iota(jnp.int32, gram.shape, 1)
    gram = gram + jnp.where(row_ids == col_ids, ridge[0], 0.0)
    factor = jnp.where(row_ids >= panel_start, mm(gram, inverse, 1, 1), 0.0)
    window = jnp.where(row >= owner, mm(cut, inverse, 1, 1), 0.0)
    updated = trailing - mm(factor, window, 1, 1)
    return lax.dynamic_slice_in_dim(factor, col * 16, 16, 0), updated


def solution(mesh):
    names = (*ROW, *COL)
    inner = Mesh(mesh.devices.reshape(8, 2, 4, 4, 2), names)
    placed = (P(ROW, COL), P(ROW, COL), P(), P())
    return jax.shard_map(
        local,
        mesh=inner,
        in_specs=placed,
        out_specs=(P(names, None), P(ROW, COL)),
        check_vma=False,
    )
```

time: 1290 us -> 150 us (0.12)
  waiting for transfers between devices: 920 us -> 15.1 us
  blocking collectives: 282 us -> 17.7 us
  starting transfers between devices: 0.16 us -> 83.5 us
  other arithmetic: 58.6 us -> 1.45 us
  Pallas kernels: 0 us -> 18.3 us
  between operations: 16.8 us -> 2.19 us
    psum x3 -> x0, waiting for transfers between devices: 636 us -> none  [spread(): return lax.psum(block, axis)]
    unnamed x5 -> x0, waiting for transfers between devices: 284 us -> none
    all_gather x2 -> x0, blocking collectives: 282 us -> none  [the longest x1 145 us: local(): factor_block = lax.all_gather(factor_mine, 'col', axis=0, tiled=True)]
    ppermute x0 -> x10, starting transfers between devices: none -> 79.9 us  [the longest x3 46.5 us: cross(): moved = lax.ppermute(block, 'zl', [(i, i ^ step) for i in range(8)])]
    another operation x9 -> x0, other arithmetic: 53.7 us -> none  [the longest x6 34 us: local(): lower = jnp.linalg.cholesky(diagonal)]
    pallas_call x0 -> x5, Pallas kernels: none -> 18.3 us  [call(): pl.pallas_call(kernel, out_shape=outs, in_specs=[vmem] * len(args), out_s...]
    all_to_all x0 -> x1, blocking collectives: none -> 17.7 us  [local(): parts = lax.all_to_all(parts, PLANE, 0, 0, tiled=True)]
  transfers between devices with their start and end apart: 4 -> 11, of which waited for: 4 -> 4; matrix products, arithmetic and copies ran while one was open for 0% -> 4% of each run, Pallas kernels for 0% -> 10%
where the time goes in v1:
time: 150 us; the launch traced here: 149 us
  starting transfers between devices  83.5 us (56%)
  Pallas kernels  18.3 us (12%)
  blocking collectives  17.7 us (12%)
  waiting for transfers between devices  15.1 us (10%)
  local copies, waits for them, and re-layouts  7.92 us (5%)
  matrix products  3.32 us (2%)
  between operations  2.19 us (1%)
    ppermute x3, starting transfers between devices, cross(): moved = lax.ppermute(block, 'zl', [(i, i ^ step) for i in range(8)])  46.5 us
    pallas_call x5, Pallas kernels, call(): pl.pallas_call(kernel, out_shape=outs, in_specs=[vmem] * len(args), out_s...  18.3 us
    all_to_all x1, blocking collectives, local(): parts = lax.all_to_all(parts, PLANE, 0, 0, tiled=True)  17.7 us
    ppermute x1, starting transfers between devices, local(): piece = piece + lax.ppermute(piece, 'zh', SWAP)  13 us
    all_to_all x1, waiting for transfers between devices, local(): lax.all_to_all(jnp.broadcast_to(piece[None], parts.shape), PLANE, 0, 0, t...  11.4 us
    ppermute x1, starting transfers between devices, local(): moved = lax.ppermute(panel, 'core', SWAP)  8.79 us
    ppermute x1, starting transfers between devices, window_and_inverse(): lax.ppermute(other, 'core', SWAP)  5.1 us
    all_to_all x1, starting transfers between devices, local(): lax.all_to_all(jnp.broadcast_to(piece[None], parts.shape), PLANE, 0, 0, t...  3.61 us
  transfers between devices with their start and end apart: 11, of which 4 were waited for; matrix products, arithmetic and copies ran while one was open for 4% of the time, Pallas kernels for 10%

profile of v1, /device:TPU:1, one launch (start us, length us, event | category | flops | bytes accessed | tf_op | source)
XLA Modules:
  0.0 149.5 jit_solution(15855532949462007928)
XLA Ops:
  1.3 1.2 constant_dynamic-slice_fusion.1
  2.5 5.3 %conditional.1 = (bf16[256,1536]{1,0:T(8,128)(2,1)}, bf16[256,1536]{1,0:T(8,128)(2,1)}, bf16[256,1536]{1,0:T(8,128)(2,1)S(1)}, s32[]{:T(128)}, s32[]{:T(128)}, /*index=5*/s32[]{:T(128)}, s32[]{:T(128)}, s32[]{:T(128)}) conditional(s32[]{:T(128)} %clamp.3, ...), branch_computations={%region_0.1_spmd, %region_1.2_spmd, %region_2.3_spmd, %region_3.4_... | conditional | flops 786446 | bytes 15729012 | solution.py:172
  2.5 0.7 collective-permute-start.15
  3.3 0.7 collective-permute-start.16
  4.1 1.0 broadcast_select_fusion.11
  5.1 1.6 %collective-permute-start.17 = (bf16[256,1536]{1,0:T(8,128)(2,1)}, bf16[256,1536]{1,0:T(8,128)(2,1)}, u32[]{:S(2)}, u32[]{:S(2)}) collective-permute-start(bf16[256,1536]{1,0:T(8,128)(2,1)} %broadcast_select_fusion.11), channel_id=1, source_target_pairs={{160,224},{416,480},{288,352},{161,225},{417,481},{289,353},{162,2... | collective-permute-start | bytes 2359304 | tf_op jit(solution)/shard_map/cond/branch_5_fun/ppermute | solution.py:30
  6.6 1.1 copy.92
  7.8 8.8 %collective-permute-start.24 = (bf16[256,1536]{1,0:T(8,128)(2,1)S(1)}, bf16[256,1536]{1,0:T(8,128)(2,1)S(1)}, u32[]{:S(2)}, u32[]{:S(2)}) collective-permute-start(bf16[256,1536]{1,0:T(8,128)(2,1)S(1)} %broadcast_select_fusion.16.own_ref), channel_id=1, source_target_pairs={{0,32},{32,0},{1,33},{33,1},{2,34},{34,2},{3,35},{35,3},{4,36},{36... | collective-permute-start | bytes 2359304 | tf_op jit(solution)/shard_map/ppermute | solution.py:173
  16.7 1.9 %collective-permute-done.24.moved_ref = bf16[256,1536]{1,0:T(8,128)(2,1)S(1)} collective-permute-done((bf16[256,1536]{1,0:T(8,128)(2,1)S(1)}, bf16[256,1536]{1,0:T(8,128)(2,1)S(1)}, u32[]{:S(2)}, u32[]{:S(2)}) %collective-permute-start.24) | collective-permute-done | bytes 786464 | tf_op jit(solution)/shard_map/ppermute | solution.py:173
  18.5 0.9 copy-done.2
  19.4 3.6 %shard_map.59 = f32[16,48,256]{2,1,0:T(8,128)} custom-call(s32[1,1]{1,0:T(1,128)} %bitcast.2.flag_ref, bf16[512,1536]{1,0:T(8,128)(2,1)} %s_ref.1, bf16[256,1536]{1,0:T(8,128)(2,1)} %copy-done, bf16[256,1536]{1,0:T(8,128)(2,1)} %copy-done.2), custom_call_target="tpu_custom_call" | custom-call | flops 1000000000 | bytes 1000000 | tf_op jit(solution)/shard_map/pallas_call | solution.py:45
  23.0 17.7 %all_to_all.10 = f32[16,48,256]{2,1,0:T(8,128)S(1)} all-to-all(f32[16,48,256]{2,1,0:T(8,128)} %shard_map.59), channel_id=1, replica_groups=mesh['zl'=8,'core'=2,'y'=4,'x'=4,'zh'=2] {'y','x'}, dimensions={0} | all-to-all | bytes 1572864 | tf_op jit(solution)/shard_map/all_to_all | solution.py:176
  40.8 13.0 %collective-permute-start.25 = (f32[48,256]{1,0:T(8,128)S(1)}, f32[48,256]{1,0:T(8,128)S(1)}, u32[]{:S(2)}, u32[]{:S(2)}) collective-permute-start(f32[48,256]{1,0:T(8,128)S(1)} %reduce_sum.9), channel_id=1, source_target_pairs={{0,1},{1,0},{2,3},{3,2},{4,5},{5,4},{6,7},{7,6},{8,9},{9,8},{10,11... | collective-permute-start | bytes 147464 | tf_op jit(solution)/shard_map/ppermute | solution.py:178
  53.7 1.5 collective-permute-done.25
  55.2 1.0 broadcast_in_dim.27
  56.2 3.6 %all-to-all-start.1 = ((f32[16,48,256]{2,1,0:T(8,128)}), f32[16,48,256]{2,1,0:T(8,128)S(1)}, u32[]{:S(2)}, u32[]{:S(2)}) async-start(f32[16,48,256]{2,1,0:T(8,128)} %broadcast_in_dim.27), calls=%async_computation.1 | async-start | bytes 1572864 | tf_op jit(solution)/shard_map/all_to_all | solution.py:179
  60.5 11.4 %all-to-all-done.1 = f32[16,48,256]{2,1,0:T(8,128)S(1)} async-done(((f32[16,48,256]{2,1,0:T(8,128)}), f32[16,48,256]{2,1,0:T(8,128)S(1)}, u32[]{:S(2)}, u32[]{:S(2)}) %all-to-all-start.1) | async-done | bytes 786464 | tf_op jit(solution)/shard_map/all_to_all | solution.py:179
  72.0 0.7 fusion.8
  73.3 5.1 %collective-permute-start.26 = (f32[64,256]{1,0:T(8,128)S(1)}, f32[64,256]{1,0:T(8,128)S(1)}, u32[]{:S(2)}, u32[]{:S(2)}) collective-permute-start(f32[64,256]{1,0:T(8,128)S(1)} %bitcast.21), channel_id=1, source_target_pairs={{0,32},{32,0},{1,33},{33,1},{2,34},{34,2},{3,35},{35,3},{4,36},{36... | collective-permute-start | bytes 196616 | tf_op jit(solution)/shard_map/ppermute | solution.py:151
  78.6 3.3 %shard_map.60 = (f32[128,128]{1,0:T(8,128)}, f32[128,128]{1,0:T(8,128)}, f32[128,128]{1,0:T(8,128)}) custom-call(f32[128,128]{1,0:T(8,128)} %get-tuple-element.53.d_ref, f32[8,128]{1,0:T(8,128)} %slice.54.after_ref), custom_call_target="tpu_custom_call" | custom-call | flops 1000000000 | bytes 1000000 | tf_op jit(solution)/shard_map/pallas_call | solution.py:45
  81.9 39.5 %collective-permute-start.27 = (f32[64,256]{1,0:T(8,128)S(1)}, f32[64,256]{1,0:T(8,128)S(1)}, u32[]{:S(2)}, u32[]{:S(2)}) collective-permute-start(f32[64,256]{1,0:T(8,128)S(1)} %bitcast_select_fusion), channel_id=1, source_target_pairs={{0,256},{64,320},{128,384},{192,448},{256,0},{320,64},{384,128},{4... | collective-permute-start | bytes 196616 | tf_op jit(solution)/shard_map/ppermute | solution.py:147
  121.4 0.6 slice.57.after_ref
  122.0 4.3 %shard_map.61 = (f32[128,128]{1,0:T(8,128)}, f32[128,128]{1,0:T(8,128)}, f32[128,128]{1,0:T(8,128)}) custom-call(f32[128,128]{1,0:T(8,128)} %get-tuple-element.39.a_ref, f32[128,128]{1,0:T(8,128)} %get-tuple-element.40.e_ref, f32[128,128]{1,0:T(8,128)} %get-tuple-element.41.m_in, f32[128,128]{1,0:T(8,128)} %get-tuple-element.52.d10_ref, ...), custom_call_target="tpu_custom_call" | custom-call | flops 1000000000 | bytes 1000000 | tf_op jit(solution)/shard_map/pallas_call | solution.py:45
  126.3 2.1 %collective-permute-start.28 = (f32[64,256]{1,0:T(8,128)S(1)}, f32[64,256]{1,0:T(8,128)S(1)}, u32[]{:S(2)}, u32[]{:S(2)}) collective-permute-start(f32[64,256]{1,0:T(8,128)S(1)} %broadcast_select_fusion.19), channel_id=1, source_target_pairs={{0,128},{64,192},{128,0},{192,64},{256,384},{320,448},{384,256},{4... | collective-permute-start | bytes 196616 | tf_op jit(solution)/shard_map/ppermute | solution.py:147
  128.4 0.6 slice.58.after_ref
  129.0 3.3 %shard_map.62 = (f32[128,128]{1,0:T(8,128)}, f32[128,128]{1,0:T(8,128)}, f32[128,128]{1,0:T(8,128)}) custom-call(f32[128,128]{1,0:T(8,128)} %get-tuple-element.42.d_ref, f32[8,128]{1,0:T(8,128)} %slice.58.after_ref), custom_call_target="tpu_custom_call" | custom-call | flops 1000000000 | bytes 1000000 | tf_op jit(solution)/shard_map/pallas_call | solution.py:45
  132.3 4.9 %collective-permute-start.29 = (f32[64,256]{1,0:T(8,128)S(1)}, f32[64,256]{1,0:T(8,128)S(1)}, u32[]{:S(2)}, u32[]{:S(2)}) collective-permute-start(f32[64,256]{1,0:T(8,128)S(1)} %broadcast_select_fusion.18), channel_id=1, source_target_pairs={{0,64},{64,0},{128,192},{192,128},{256,320},{320,256},{384,448},{4... | collective-permute-start | bytes 196616 | tf_op jit(solution)/shard_map/ppermute | solution.py:147
  137.8 3.9 %shard_map.63 = (f32[256,256]{1,0:T(8,128)}, f32[128,128]{1,0:T(8,128)}) custom-call(f32[128,128]{1,0:T(8,128)} %get-tuple-element.43.a_ref, f32[128,128]{1,0:T(8,128)} %get-tuple-element.44.e_ref, f32[128,128]{1,0:T(8,128)} %get-tuple-element.45.m_in, f32[128,128]{1,0:T(8,128)} %get-tuple-element.46.m00_ref, f32[128,128]{1,0:T(8,128)} %get-tuple-element.47.x_ref, ...), custom_call_target="tpu_custom_call" | custom-call | flops 1000000000 | bytes 1000000 | tf_op jit(solution)/shard_map/pallas_call | solution.py:45
  141.7 1.6 %convolution_select_fusion = f32[512,256]{1,0:T(8,128)S(1)} fusion(f32[512,256]{1,0:T(8,128)S(1)} %bitcast_add_fusion, f32[256,256]{1,0:T(8,128)} %get-tuple-element.48, pred[512]{0:T(512)(128)(4,1)S(1)} %broadcast_compare_fusion), kind=kOutput, calls=%fused_computation.16 | convolution fusion | flops 402784256 | bytes 1311232 | tf_op jit(solution)/shard_map/dot_general | solution.py:39
  143.3 3.5 %collective-permute-start.30 = (f32[64,256]{1,0:T(8,128)S(1)}, f32[64,256]{1,0:T(8,128)S(1)}, u32[]{:S(2)}, u32[]{:S(2)}) collective-permute-start(f32[64,256]{1,0:T(8,128)S(1)} %broadcast_select_fusion.17), channel_id=1, source_target_pairs={{0,32},{32,0},{1,33},{33,1},{2,34},{34,2},{3,35},{35,3},{4,36},{36... | collective-permute-start | bytes 196616 | tf_op jit(solution)/shard_map/ppermute | solution.py:159
  146.9 0.6 constant_dynamic-slice_fusion
  148.2 1.3 convolution_subtract_fusion
  (34 shorter events, 2.4 us)
Async XLA Ops:
  2.5 0.7 collective-permute-start.15
  3.3 0.7 collective-permute-start.16
  5.1 2.7 %collective-permute-start.17 = (bf16[256,1536]{1,0:T(8,128)(2,1)}, bf16[256,1536]{1,0:T(8,128)(2,1)}, u32[]{:S(2)}, u32[]{:S(2)}) collective-permute-start(bf16[256,1536]{1,0:T(8,128)(2,1)} %broadcast_select_fusion.11), channel_id=1, source_target_pairs={{160,224},{416,480},{288,352},{161,225},{417,481},{289,353},{162,2... | collective-permute-start | bytes 2359304 | tf_op jit(solution)/shard_map/cond/branch_5_fun/ppermute | solution.py:30
  7.8 10.7 %copy-start = (bf16[256,1536]{1,0:T(8,128)(2,1)}, bf16[256,1536]{1,0:T(8,128)(2,1)S(1)}, u32[]{:S(2)}) copy-start(bf16[256,1536]{1,0:T(8,128)(2,1)S(1)} %broadcast_select_fusion.16.own_ref) | copy-start | bytes 2359300
  7.8 10.7 %collective-permute-start.24 = (bf16[256,1536]{1,0:T(8,128)(2,1)S(1)}, bf16[256,1536]{1,0:T(8,128)(2,1)S(1)}, u32[]{:S(2)}, u32[]{:S(2)}) collective-permute-start(bf16[256,1536]{1,0:T(8,128)(2,1)S(1)} %broadcast_select_fusion.16.own_ref), channel_id=1, source_target_pairs={{0,32},{32,0},{1,33},{33,1},{2,34},{34,2},{3,35},{35,3},{4,36},{36... | collective-permute-start | bytes 2359304 | tf_op jit(solution)/shard_map/ppermute | solution.py:173
  18.5 0.9 copy-start.2
  40.8 14.4 %collective-permute-start.25 = (f32[48,256]{1,0:T(8,128)S(1)}, f32[48,256]{1,0:T(8,128)S(1)}, u32[]{:S(2)}, u32[]{:S(2)}) collective-permute-start(f32[48,256]{1,0:T(8,128)S(1)} %reduce_sum.9), channel_id=1, source_target_pairs={{0,1},{1,0},{2,3},{3,2},{4,5},{5,4},{6,7},{7,6},{8,9},{9,8},{10,11... | collective-permute-start | bytes 147464 | tf_op jit(solution)/shard_map/ppermute | solution.py:178
  56.2 15.8 %all-to-all-start.1 = ((f32[16,48,256]{2,1,0:T(8,128)}), f32[16,48,256]{2,1,0:T(8,128)S(1)}, u32[]{:S(2)}, u32[]{:S(2)}) async-start(f32[16,48,256]{2,1,0:T(8,128)} %broadcast_in_dim.27), calls=%async_computation.1 | async-start | bytes 1572864 | tf_op jit(solution)/shard_map/all_to_all | solution.py:179
  73.3 8.6 %collective-permute-start.26 = (f32[64,256]{1,0:T(8,128)S(1)}, f32[64,256]{1,0:T(8,128)S(1)}, u32[]{:S(2)}, u32[]{:S(2)}) collective-permute-start(f32[64,256]{1,0:T(8,128)S(1)} %bitcast.21), channel_id=1, source_target_pairs={{0,32},{32,0},{1,33},{33,1},{2,34},{34,2},{3,35},{35,3},{4,36},{36... | collective-permute-start | bytes 196616 | tf_op jit(solution)/shard_map/ppermute | solution.py:151
  81.9 44.3 %collective-permute-start.27 = (f32[64,256]{1,0:T(8,128)S(1)}, f32[64,256]{1,0:T(8,128)S(1)}, u32[]{:S(2)}, u32[]{:S(2)}) collective-permute-start(f32[64,256]{1,0:T(8,128)S(1)} %bitcast_select_fusion), channel_id=1, source_target_pairs={{0,256},{64,320},{128,384},{192,448},{256,0},{320,64},{384,128},{4... | collective-permute-start | bytes 196616 | tf_op jit(solution)/shard_map/ppermute | solution.py:147
  126.3 6.0 %collective-permute-start.28 = (f32[64,256]{1,0:T(8,128)S(1)}, f32[64,256]{1,0:T(8,128)S(1)}, u32[]{:S(2)}, u32[]{:S(2)}) collective-permute-start(f32[64,256]{1,0:T(8,128)S(1)} %broadcast_select_fusion.19), channel_id=1, source_target_pairs={{0,128},{64,192},{128,0},{192,64},{256,384},{320,448},{384,256},{4... | collective-permute-start | bytes 196616 | tf_op jit(solution)/shard_map/ppermute | solution.py:147
  132.3 11.1 %collective-permute-start.29 = (f32[64,256]{1,0:T(8,128)S(1)}, f32[64,256]{1,0:T(8,128)S(1)}, u32[]{:S(2)}, u32[]{:S(2)}) collective-permute-start(f32[64,256]{1,0:T(8,128)S(1)} %broadcast_select_fusion.18), channel_id=1, source_target_pairs={{0,64},{64,0},{128,192},{192,128},{256,320},{320,256},{384,448},{4... | collective-permute-start | bytes 196616 | tf_op jit(solution)/shard_map/ppermute | solution.py:147
  141.7 6.1 %copy-start.1 = (f32[256,256]{1,0:T(8,128)S(1)}, f32[256,256]{1,0:T(8,128)}, u32[]{:S(2)}) copy-start(f32[256,256]{1,0:T(8,128)} %get-tuple-element.48) | copy-start | bytes 786436
  141.7 6.5 %copy-start.3 = (f32[512,128]{1,0:T(8,128)S(1)}, f32[512,128]{1,0:T(8,128)}, u32[]{:S(2)}) copy-start(f32[512,128]{1,0:T(8,128)} %param.13) | copy-start | bytes 786436
  143.3 4.4 %collective-permute-start.30 = (f32[64,256]{1,0:T(8,128)S(1)}, f32[64,256]{1,0:T(8,128)S(1)}, u32[]{:S(2)}, u32[]{:S(2)}) collective-permute-start(f32[64,256]{1,0:T(8,128)S(1)} %broadcast_select_fusion.17), channel_id=1, source_target_pairs={{0,32},{32,0},{1,33},{33,1},{2,34},{34,2},{3,35},{35,3},{4,36},{36... | collective-permute-start | bytes 196616 | tf_op jit(solution)/shard_map/ppermute | solution.py:159

commit v2 on v1

--- a/solution.py
+++ b/solution.py
@@ -16,21 +16,24 @@
 F32 = jnp.float32
 
 
-def member(ids, position):
-    bits = sum(1 << i for i in ids)
-    return (jnp.int32(bits) >> position) & 1 == 1
-
-
-def panel_tree(owner):
-    def branch(own):
-        row = lax.axis_index(ROW)
-        held, block = [owner], own
-        for step in (8, 4, 2):
-            pairs = [(h, h + step) for h in held if h + step < ROWS]
-            moved = lax.ppermute(block, ROW, pairs)
-            block = jnp.where(member([t for _, t in pairs], row), moved, block)
-            held = held + [t for _, t in pairs]
-        return block
+def panel_tree(first):
+    def branch(*pieces):
+        zl = lax.axis_index("zl")
+        far, back, on = first + 4, first + 2, first + 6
+        last = [(i, i + 1) for i in range(first & 1, 7, 2)]
+        out = []
+        for piece in pieces:
+            moved = lax.ppermute(piece, "zl", [(first, far)])
+            piece = jnp.where(zl == far, moved, piece)
+            moved = lax.ppermute(piece, "zl", [(far, back)])
+            if on < 8:
+                onward = lax.ppermute(piece, "zl", [(far, on)])
+                piece = jnp.where(zl == on, onward, piece)
+            piece = jnp.where(zl == back, moved, piece)
+            moved = lax.ppermute(piece, "zl", last)
+            piece = jnp.where((zl - first) & 1 == 1, moved, piece)
+            out.append(lax.all_gather(piece, "core"))
+        return out
 
     return branch
 
@@ -39,7 +42,7 @@
     return lax.dot_general(a, b, (((ca,), (cb,)), ((), ())), precision=HIGHEST, preferred_element_type=F32)
 
 
-def call(kernel, outs, *args, flops=10**9):
+def call(kernel, outs, *args, flops=10**9, room=4 << 20):
     cost = pl.CostEstimate(flops=flops, bytes_accessed=10**6, transcendentals=0)
     vmem = pl.BlockSpec(memory_space=pltpu.VMEM)
     return pl.pallas_call(
@@ -48,17 +51,20 @@
         in_specs=[vmem] * len(args),
         out_specs=(vmem,) * len(outs) if isinstance(outs, tuple) else vmem,
         cost_estimate=cost,
+        compiler_params=pltpu.CompilerParams(vmem_limit_bytes=room),
     )(*args)
 
 
-def gram_kernel(flag_ref, s_ref, own_ref, moved_ref, out_ref):
-    panel = jnp.where(flag_ref[...] > 0, own_ref[...], moved_ref[...])
+def gram_kernel(core_ref, s_ref, low_ref, high_ref, out_ref):
+    halves = [jnp.concatenate([low_ref[i], high_ref[i]]) for i in range(2)]
+    half = jnp.where(core_ref[...] == 0, halves[0], halves[1])
+    panel = jnp.concatenate(halves)
     dims = (((1,), (1,)), ((), ()))
     gram = lax.dot_general(s_ref[...], panel, dims, preferred_element_type=F32)
-    diag = lax.dot_general(panel, panel, dims, preferred_element_type=F32)
+    diag = lax.dot_general(half, panel, dims, preferred_element_type=F32)
     for k in range(16):
         out_ref[k, :32, :] = gram[32 * k : 32 * k + 32]
-        out_ref[k, 32:, :] = diag[16 * k : 16 * k + 16]
+        out_ref[k, 32:, :] = diag[8 * k : 8 * k + 8]
 
 
 def rsqrt(v):
@@ -136,7 +142,7 @@
 FULL = jax.ShapeDtypeStruct((PANEL, PANEL), F32)
 
 
-def window_and_inverse(cut, source, diag):
+def window_and_inverse(cut, source, diag_half, prepare):
     zl, core = lax.axis_index("zl"), lax.axis_index("core")
     rows = cut.shape[0] // 2
     halves = cut.reshape(2, rows, PANEL)
@@ -148,16 +154,18 @@
         return jnp.where((zl ^ (source >> 1)) & step != 0, moved, block)
 
     token = lambda v: v[:8, :HALF]
-    block = jnp.where(core == (source & 1), mine, lax.ppermute(other, "core", SWAP))
-    a, e, m = call(start_block, (SQUARE,) * 3, diag[:HALF, :HALF], token(diag))
+    both = lax.all_gather(jnp.concatenate([diag_half, other]), "core")
+    diag = prepare(both[:, :HALF].reshape(PANEL, PANEL))
+    moved = jnp.where(core == 0, both[1, HALF:], both[0, HALF:])
+    block = jnp.where(core == (source & 1), mine, moved)
     far = cross(block, 4)
+    a, e, m = call(start_block, (SQUARE,) * 3, diag[:HALF, :HALF], token(block))
     m00, x, d11 = call(end_upper, (SQUARE,) * 3, a, e, m, diag[HALF:, :HALF], diag[HALF:, HALF:], token(block))
+    a, e, m = call(start_block, (SQUARE,) * 3, d11, token(block))
     mid = cross(far, 2)
-    a, e, m = call(start_block, (SQUARE,) * 3, d11, token(far))
-    near = cross(mid, 1)
-    inverse = call(end_lower, (FULL, SQUARE), a, e, m, m00, x, token(mid))[0]
-    moved = lax.ppermute(near, "core", SWAP)
-    return jnp.where(core == 0, jnp.concatenate([near, moved]), jnp.concatenate([moved, near])), inverse
+    inverse = call(end_lower, (FULL, SQUARE), a, e, m, m00, x, token(far))[0]
+    four = lax.all_gather(mid, ROW, axis_index_groups=[[i, i + 1, i + 2, i + 3] for i in range(0, ROWS, 4)])
+    return jnp.where((source >> 1) & 1 == 0, four[:2], four[2:]).reshape(cut.shape), inverse
 
 
 def local(signatures, trailing, ridge, panel_index):
@@ -168,22 +176,30 @@
     index = panel_index[0]
     panel_start = index * PANEL
     owner = index >> 1
-    own = lax.dynamic_slice_in_dim(signatures, panel_start & (rows_dev - 1), PANEL, 0)
-    panel = lax.switch(owner, [panel_tree(o) for o in range(8)], own)
-    moved = lax.ppermute(panel, "core", SWAP)
-    flag = jnp.full((1, 1), core == (owner & 1), jnp.int32)
-    parts = call(gram_kernel, jax.ShapeDtypeStruct((16, 48, PANEL), F32), flag, signatures, panel, moved)
+    offset = panel_start & (rows_dev - 1)
+    mine = lax.dynamic_slice_in_dim(signatures, offset + HALF * core, HALF, 0)
+    other = lax.dynamic_slice_in_dim(signatures, offset + HALF * (1 - core), HALF, 0)
+    half = jnp.where(core == (owner & 1), mine, lax.ppermute(other, "core", SWAP))
+    low, high = lax.switch(owner >> 1, [panel_tree(i) for i in range(4)], half[: HALF // 2], half[HALF // 2 :])
+    parts = call(
+        gram_kernel,
+        jax.ShapeDtypeStruct((16, 40, PANEL), F32),
+        jnp.full((1, 1), core, jnp.int32),
+        signatures,
+        low,
+        high,
+        room=16 << 20,
+    )
     parts = lax.all_to_all(parts, PLANE, 0, 0, tiled=True)
-    piece = jnp.sum(parts, axis=0)
-    piece = piece + lax.ppermute(piece, "zh", SWAP)
+    piece = jnp.sum(lax.all_gather(jnp.sum(parts, axis=0), "zh"), axis=0)
     pieces = lax.all_to_all(jnp.broadcast_to(piece[None], parts.shape), PLANE, 0, 0, tiled=True)
 
     cut_start = 8 * ((index + 1 + x) & 1) + 4 * zh
     cut = lax.dynamic_slice_in_dim(pieces, cut_start, 4, 0)[:, :32].reshape(tile_cols, PANEL)
-    diag = pieces[:, 32:].reshape(PANEL, PANEL)
     eye = jnp.eye(PANEL, dtype=F32)
-    diag = jnp.where(row >= owner, diag + ridge[0] * eye, eye)
-    cut, inverse = window_and_inverse(cut, 2 * y + ((index + 1 + x) >> 1), diag)
+    prepare = lambda diag: jnp.where(row >= owner, diag + ridge[0] * eye, eye)
+    source = 2 * y + ((index + 1 + x) >> 1)
+    cut, inverse = window_and_inverse(cut, source, pieces[:, 32:].reshape(HALF, PANEL), prepare)
 
     gram = pieces[:, :32].reshape(rows_dev, PANEL)
     row_ids = row * rows_dev + lax.broadcasted_iota(jnp.int32, gram.shape, 0)

time: 150 us -> 126 us (0.84)
  starting transfers between devices: 83.5 us -> 42 us
  blocking collectives: 17.7 us -> 49.4 us
  Pallas kernels: 18.3 us -> 9.66 us
  local copies, waits for them, and re-layouts: 7.92 us -> 2.68 us
    all_gather x0 -> x5, blocking collectives: none -> 33.5 us  [the longest x1 14.7 us: local(): piece = jnp.sum(lax.all_gather(jnp.sum(parts, axis=0), 'zh'), axis=0)]
    ppermute x3 -> x2, starting transfers between devices: 46.5 us -> 24.2 us  [cross(): moved = lax.ppermute(block, 'zl', [(i, i ^ step) for i in range(8)])]
    ppermute x7, starting transfers between devices: 33.4 us -> 14.2 us  [the longest x1 8.79 us: local(): half = jnp.where(core == owner & 1, mine, lax.ppermute(other, 'core', SWAP))]
    pallas_call x5, Pallas kernels: 18.3 us -> 9.66 us  [call(): pl.pallas_call(kernel, out_shape=outs, in_specs=[vmem] * len(args), out_s...]
    slice x4 -> x2, local copies, waits for them, and re-layouts: 2.38 us -> 0.01 us  [window_and_inverse(): token = lambda v: v[:8, :HALF]]
    all_to_all x1, blocking collectives: 17.7 us -> 15.9 us  [local(): parts = lax.all_to_all(parts, PLANE, 0, 0, tiled=True)]
    ppermute x7, waiting for transfers between devices: 3.62 us -> 5.28 us  [the longest x2 3.96 us: branch(): moved = lax.ppermute(piece, 'zl', last)]
  transfers between devices with their start and end apart: 11 -> 10, of which waited for: 4 -> 5; matrix products, arithmetic and copies ran while one was open for 4% -> 1% of each run, Pallas kernels for 10% -> 7%
where the time goes in v2:
time: 126 us; the launch traced here: 125 us
  blocking collectives  49.4 us (39%)
  starting transfers between devices  42 us (33%)
  waiting for transfers between devices  15.5 us (12%)
  Pallas kernels  9.66 us (8%)
  local copies, waits for them, and re-layouts  2.68 us (2%)
  matrix products  2.3 us (2%)
  between operations  2.22 us (2%)
  other arithmetic  1.54 us (1%)
    ppermute x2, starting transfers between devices, cross(): moved = lax.ppermute(block, 'zl', [(i, i ^ step) for i in range(8)])  24.2 us
    all_to_all x1, blocking collectives, local(): parts = lax.all_to_all(parts, PLANE, 0, 0, tiled=True)  15.9 us
    all_gather x1, blocking collectives, local(): piece = jnp.sum(lax.all_gather(jnp.sum(parts, axis=0), 'zh'), axis=0)  14.7 us
    all_to_all x1, waiting for transfers between devices, local(): lax.all_to_all(jnp.broadcast_to(piece[None], parts.shape), PLANE, 0, 0, t...  10.2 us
    pallas_call x5, Pallas kernels, call(): pl.pallas_call(kernel, out_shape=outs, in_specs=[vmem] * len(args), out_s...  9.66 us
    ppermute x1, starting transfers between devices, local(): half = jnp.where(core == owner & 1, mine, lax.ppermute(other, 'core', SWAP))  8.79 us
    all_gather x1, blocking collectives, window_and_inverse(): lax.all_gather(mid, ROW, axis_index_groups=[[i, i + 1, i + 2, i + 3] for...  8.41 us
    all_gather x2, blocking collectives, branch(): out.append(lax.all_gather(piece, 'core'))  5.68 us
  transfers between devices with their start and end apart: 10, of which 5 were waited for; matrix products, arithmetic and copies ran while one was open for 1% of the time, Pallas kernels for 7%

profile of v2, /device:TPU:1, one launch (start us, length us, event | category | flops | bytes accessed | tf_op | source)
XLA Modules:
  0.0 125.5 jit_solution(1905873134822288485)
XLA Ops:
  1.3 1.0 constant_dynamic-slice_fusion.1
  2.3 8.8 %collective-permute-start.28 = (bf16[128,1536]{1,0:T(8,128)(2,1)S(1)}, bf16[128,1536]{1,0:T(8,128)(2,1)S(1)}, u32[]{:S(2)}, u32[]{:S(2)}) collective-permute-start(bf16[128,1536]{1,0:T(8,128)(2,1)S(1)} %constant_dynamic-slice_fusion.1), channel_id=1, source_target_pairs={{0,32},{32,0},{1,33},{33,1},{2,34},{34,2},{3,35},{35,3},{4,36},{36... | collective-permute-start | bytes 1179656 | tf_op jit(solution)/shard_map/ppermute | solution.py:182
  11.1 1.3 %collective-permute-done.28 = bf16[128,1536]{1,0:T(8,128)(2,1)S(1)} collective-permute-done((bf16[128,1536]{1,0:T(8,128)(2,1)S(1)}, bf16[128,1536]{1,0:T(8,128)(2,1)S(1)}, u32[]{:S(2)}, u32[]{:S(2)}) %collective-permute-start.28) | collective-permute-done | bytes 393248 | tf_op jit(solution)/shard_map/ppermute | solution.py:182
  12.4 1.1 dynamic-slice_select_fusion
  13.6 15.4 %conditional.1 = (bf16[2,64,1536]{2,1,0:T(8,128)(2,1)S(1)}, bf16[2,64,1536]{2,1,0:T(8,128)(2,1)S(1)}) conditional(s32[]{:T(128)} %clamp.3, (bf16[64,1536]{1,0:T(8,128)(2,1)S(1)}, bf16[64,1536]{1,0:T(8,128)(2,1)S(1)}) %tuple.24, (bf16[64,1536]{1,0:T(8,128)(2,1)S(1)}, bf16[64,1536]{1,0:T(8,128)(2,1)S(1)}) %tuple.24, ...), branch_computations={%region_0.1_spmd, %region_1.2_spmd, %region_2.3_spmd, %region_3.4_... | conditional | flops 786441 | bytes 11403700 | solution.py:183
  13.6 0.8 collective-permute-start.19
  14.4 0.7 collective-permute-start.16
  15.1 0.7 collective-permute-start.20
  15.9 0.7 collective-permute-start.17
  16.6 1.3 %collective-permute-start.21 = (bf16[64,1536]{1,0:T(8,128)(2,1)S(1)}, bf16[64,1536]{1,0:T(8,128)(2,1)S(1)}, u32[]{:S(2)}, u32[]{:S(2)}) collective-permute-start(bf16[64,1536]{1,0:T(8,128)(2,1)S(1)} %broadcast_select_fusion.10), channel_id=1, source_target_pairs={{0,64},{128,192},{256,320},{384,448},{1,65},{129,193},{257,321},{3... | collective-permute-start | bytes 589832 | tf_op jit(solution)/shard_map/cond/branch_2_fun/ppermute | solution.py:33
  17.9 1.3 %collective-permute-start.18 = (bf16[64,1536]{1,0:T(8,128)(2,1)S(1)}, bf16[64,1536]{1,0:T(8,128)(2,1)S(1)}, u32[]{:S(2)}, u32[]{:S(2)}) collective-permute-start(bf16[64,1536]{1,0:T(8,128)(2,1)S(1)} %broadcast_select_fusion.11), channel_id=1, source_target_pairs={{0,64},{128,192},{256,320},{384,448},{1,65},{129,193},{257,321},{3... | collective-permute-start | bytes 589832 | tf_op jit(solution)/shard_map/cond/branch_2_fun/ppermute | solution.py:33
  19.3 2.9 %collective-permute-done.21 = bf16[64,1536]{1,0:T(8,128)(2,1)S(1)} collective-permute-done((bf16[64,1536]{1,0:T(8,128)(2,1)S(1)}, bf16[64,1536]{1,0:T(8,128)(2,1)S(1)}, u32[]{:S(2)}, u32[]{:S(2)}) %collective-permute-start.21) | collective-permute-done | bytes 196640 | tf_op jit(solution)/shard_map/cond/branch_2_fun/ppermute | solution.py:33
  22.1 3.1 %all-gather.5 = bf16[128,1536]{1,0:T(8,128)(2,1)S(1)} all-gather(bf16[64,1536]{1,0:T(8,128)(2,1)S(1)} %broadcast_select_fusion.12), channel_id=7, replica_groups=mesh['zl'=8,'core'=2,'y'=4,'x'=4,'zh'=2] {'core'}, dimensions={0}, use_global_device_ids=true | all-gather | bytes 589824 | tf_op jit(solution)/shard_map/cond/branch_2_fun/all_gather | solution.py:35
  25.2 1.1 collective-permute-done.18
  26.4 2.6 %all-gather.4 = bf16[128,1536]{1,0:T(8,128)(2,1)S(1)} all-gather(bf16[64,1536]{1,0:T(8,128)(2,1)S(1)} %broadcast_select_fusion.13), channel_id=6, replica_groups=mesh['zl'=8,'core'=2,'y'=4,'x'=4,'zh'=2] {'core'}, dimensions={0}, use_global_device_ids=true | all-gather | bytes 589824 | tf_op jit(solution)/shard_map/cond/branch_2_fun/all_gather | solution.py:35
  29.0 0.8 shard_map.59
  29.8 15.9 %all_to_all.10 = f32[16,40,256]{2,1,0:T(8,128)S(1)} all-to-all(f32[16,40,256]{2,1,0:T(8,128)S(1)} %shard_map.59), channel_id=1, replica_groups=mesh['zl'=8,'core'=2,'y'=4,'x'=4,'zh'=2] {'y','x'}, dimensions={0} | all-to-all | bytes 1310720 | tf_op jit(solution)/shard_map/all_to_all | solution.py:193
  45.7 14.7 %all-gather.8 = f32[80,256]{1,0:T(8,128)S(1)} all-gather(f32[40,256]{1,0:T(8,128)S(1)} %reduce_sum.18), channel_id=10, replica_groups=mesh['zl'=8,'core'=2,'y'=4,'x'=4,'zh'=2] {'zh'}, dimensions={0}, use_global_device_ids=true | all-gather | bytes 122880 | tf_op jit(solution)/shard_map/all_gather | solution.py:194
  60.4 0.9 broadcast_in_dim.24
  61.3 3.6 %all-to-all-start.1 = ((f32[16,40,256]{2,1,0:T(8,128)}), f32[16,40,256]{2,1,0:T(8,128)S(1)}, u32[]{:S(2)}, u32[]{:S(2)}) async-start(f32[16,40,256]{2,1,0:T(8,128)} %broadcast_in_dim.24), calls=%async_computation.1 | async-start | bytes 1310720 | tf_op jit(solution)/shard_map/all_to_all | solution.py:195
  65.6 10.2 %all-to-all-done.1 = f32[16,40,256]{2,1,0:T(8,128)S(1)} async-done(((f32[16,40,256]{2,1,0:T(8,128)}), f32[16,40,256]{2,1,0:T(8,128)S(1)}, u32[]{:S(2)}, u32[]{:S(2)}) %all-to-all-start.1) | async-done | bytes 655392 | tf_op jit(solution)/shard_map/all_to_all | solution.py:195
  75.8 4.7 %all-gather.9 = f32[384,256]{1,0:T(8,128)S(1)} all-gather(f32[192,256]{1,0:T(8,128)S(1)} %pad_maximum_fusion), channel_id=11, replica_groups=mesh['zl'=8,'core'=2,'y'=4,'x'=4,'zh'=2] {'core'}, dimensions={0}, use_global_device_ids=true | all-gather | bytes 589824 | tf_op jit(solution)/shard_map/all_gather | solution.py:157
  80.6 21.8 %collective-permute-start.29 = (f32[64,256]{1,0:T(8,128)S(1)}, f32[64,256]{1,0:T(8,128)S(1)}, u32[]{:S(2)}, u32[]{:S(2)}) collective-permute-start(f32[64,256]{1,0:T(8,128)S(1)} %fusion.3), channel_id=1, source_target_pairs={{0,256},{64,320},{128,384},{192,448},{256,0},{320,64},{384,128},{4... | collective-permute-start | bytes 196616 | tf_op jit(solution)/shard_map/ppermute | solution.py:153
  102.5 1.8 %shard_map.60 = (f32[128,128]{1,0:T(8,128)S(1)}, f32[128,128]{1,0:T(8,128)S(1)}, f32[128,128]{1,0:T(8,128)S(1)}) custom-call(f32[128,128]{1,0:T(8,128)S(1)} %get-tuple-element.56.d_ref, f32[8,128]{1,0:T(8,128)S(1)} %slice.83.after_ref), custom_call_target="tpu_custom_call" | custom-call | flops 1000000000 | bytes 1000000 | tf_op jit(solution)/shard_map/pallas_call | solution.py:48
  104.4 2.7 %shard_map.61 = (f32[128,128]{1,0:T(8,128)S(1)}, f32[128,128]{1,0:T(8,128)S(1)}, f32[128,128]{1,0:T(8,128)S(1)}) custom-call(f32[128,128]{1,0:T(8,128)S(1)} %get-tuple-element.40.a_ref, f32[128,128]{1,0:T(8,128)S(1)} %get-tuple-element.41.e_ref, f32[128,128]{1,0:T(8,128)S(1)} %get-tuple-element.42.m_in, f32[128,128]{1,0:T(8,128)S(1)} %get-tuple-element.55.d10_ref, ...), custom_call_target="tpu_custom_call" | custom-call | flops 1000000000 | bytes 1000000 | tf_op jit(solution)/shard_map/pallas_call | solution.py:48
  107.1 1.8 %shard_map.62 = (f32[128,128]{1,0:T(8,128)S(1)}, f32[128,128]{1,0:T(8,128)S(1)}, f32[128,128]{1,0:T(8,128)S(1)}) custom-call(f32[128,128]{1,0:T(8,128)S(1)} %get-tuple-element.43.d_ref, f32[8,128]{1,0:T(8,128)S(1)} %slice.83.after_ref), custom_call_target="tpu_custom_call" | custom-call | flops 1000000000 | bytes 1000000 | tf_op jit(solution)/shard_map/pallas_call | solution.py:48
  109.0 2.4 %collective-permute-start.30 = (f32[64,256]{1,0:T(8,128)S(1)}, f32[64,256]{1,0:T(8,128)S(1)}, u32[]{:S(2)}, u32[]{:S(2)}) collective-permute-start(f32[64,256]{1,0:T(8,128)S(1)} %broadcast_select_fusion.21), channel_id=1, source_target_pairs={{0,128},{64,192},{128,0},{192,64},{256,384},{320,448},{384,256},{4... | collective-permute-start | bytes 196616 | tf_op jit(solution)/shard_map/ppermute | solution.py:153
  111.4 2.7 %shard_map.63 = (f32[256,256]{1,0:T(8,128)S(1)}, f32[128,128]{1,0:T(8,128)}) custom-call(f32[128,128]{1,0:T(8,128)S(1)} %get-tuple-element.44.a_ref, f32[128,128]{1,0:T(8,128)S(1)} %get-tuple-element.45.e_ref, f32[128,128]{1,0:T(8,128)S(1)} %get-tuple-element.46.m_in, f32[128,128]{1,0:T(8,128)S(1)} %get-tuple-element.47.m00_ref, ...), custom_call_target="tpu_custom_call" | custom-call | flops 1000000000 | bytes 1000000 | tf_op jit(solution)/shard_map/pallas_call | solution.py:48
  114.1 0.6 convolution_select_fusion
  114.7 0.6 constant_dynamic-slice_fusion
  115.3 8.4 %all-gather.10 = f32[256,256]{1,0:T(8,128)S(1)} all-gather(f32[64,256]{1,0:T(8,128)S(1)} %broadcast_select_fusion.20), channel_id=12, replica_groups={{0,32,64,96},{128,160,192,224},{256,288,320,352},{384,416,448,480},{1,3..., dimensions={0}, use_global_device_ids=true | all-gather | bytes 327680 | tf_op jit(solution)/shard_map/all_gather | solution.py:167
  124.2 1.3 %convolution_subtract_fusion = f32[512,128]{1,0:T(8,128)} fusion(f32[512,128]{1,0:T(8,128)S(1)} %copy-done.1, f32[512,256]{1,0:T(8,128)S(1)} %convolution_select_fusion, f32[128,256]{1,0:T(8,128)S(1)} %convolution_select_fusion.1), kind=kOutput, calls=%fused_computation.25 | convolution fusion | flops 201392128 | bytes 1179648 | tf_op jit(solution)/shard_map/dot_general | solution.py:42
  (36 shorter events, 1.1 us)
Async XLA Ops:
  2.3 10.1 %collective-permute-start.28 = (bf16[128,1536]{1,0:T(8,128)(2,1)S(1)}, bf16[128,1536]{1,0:T(8,128)(2,1)S(1)}, u32[]{:S(2)}, u32[]{:S(2)}) collective-permute-start(bf16[128,1536]{1,0:T(8,128)(2,1)S(1)} %constant_dynamic-slice_fusion.1), channel_id=1, source_target_pairs={{0,32},{32,0},{1,33},{33,1},{2,34},{34,2},{3,35},{35,3},{4,36},{36... | collective-permute-start | bytes 1179656 | tf_op jit(solution)/shard_map/ppermute | solution.py:182
  13.6 15.4 %copy-start = (bf16[512,1536]{1,0:T(8,128)(2,1)S(1)}, bf16[512,1536]{1,0:T(8,128)(2,1)}, u32[]{:S(2)}) copy-start(bf16[512,1536]{1,0:T(8,128)(2,1)} %s_ref.1) | copy-start | bytes 4718596
  13.6 1.5 %collective-permute-start.19 = (bf16[64,1536]{1,0:T(8,128)(2,1)S(1)}, bf16[64,1536]{1,0:T(8,128)(2,1)S(1)}, u32[]{:S(2)}, u32[]{:S(2)}) collective-permute-start(bf16[64,1536]{1,0:T(8,128)(2,1)S(1)} %get-tuple-element.21), channel_id=1, source_target_pairs={{128,384},{129,385},{130,386},{131,387},{132,388},{133,389},{134,3... | collective-permute-start | bytes 589832 | tf_op jit(solution)/shard_map/cond/branch_2_fun/ppermute | solution.py:26
  14.4 1.4 %collective-permute-start.16 = (bf16[64,1536]{1,0:T(8,128)(2,1)S(1)}, bf16[64,1536]{1,0:T(8,128)(2,1)S(1)}, u32[]{:S(2)}, u32[]{:S(2)}) collective-permute-start(bf16[64,1536]{1,0:T(8,128)(2,1)S(1)} %get-tuple-element.20), channel_id=1, source_target_pairs={{128,384},{129,385},{130,386},{131,387},{132,388},{133,389},{134,3... | collective-permute-start | bytes 589832 | tf_op jit(solution)/shard_map/cond/branch_2_fun/ppermute | solution.py:26
  15.1 1.4 %collective-permute-start.20 = (bf16[64,1536]{1,0:T(8,128)(2,1)S(1)}, bf16[64,1536]{1,0:T(8,128)(2,1)S(1)}, u32[]{:S(2)}, u32[]{:S(2)}) collective-permute-start(bf16[64,1536]{1,0:T(8,128)(2,1)S(1)} %broadcast_select_fusion.8), channel_id=1, source_target_pairs={{384,256},{385,257},{386,258},{387,259},{388,260},{389,261},{390,2... | collective-permute-start | bytes 589832 | tf_op jit(solution)/shard_map/cond/branch_2_fun/ppermute | solution.py:28
  15.9 2.0 %collective-permute-start.17 = (bf16[64,1536]{1,0:T(8,128)(2,1)S(1)}, bf16[64,1536]{1,0:T(8,128)(2,1)S(1)}, u32[]{:S(2)}, u32[]{:S(2)}) collective-permute-start(bf16[64,1536]{1,0:T(8,128)(2,1)S(1)} %broadcast_select_fusion.9), channel_id=1, source_target_pairs={{384,256},{385,257},{386,258},{387,259},{388,260},{389,261},{390,2... | collective-permute-start | bytes 589832 | tf_op jit(solution)/shard_map/cond/branch_2_fun/ppermute | solution.py:28
  16.6 5.5 %collective-permute-start.21 = (bf16[64,1536]{1,0:T(8,128)(2,1)S(1)}, bf16[64,1536]{1,0:T(8,128)(2,1)S(1)}, u32[]{:S(2)}, u32[]{:S(2)}) collective-permute-start(bf16[64,1536]{1,0:T(8,128)(2,1)S(1)} %broadcast_select_fusion.10), channel_id=1, source_target_pairs={{0,64},{128,192},{256,320},{384,448},{1,65},{129,193},{257,321},{3... | collective-permute-start | bytes 589832 | tf_op jit(solution)/shard_map/cond/branch_2_fun/ppermute | solution.py:33
  17.9 8.4 %collective-permute-start.18 = (bf16[64,1536]{1,0:T(8,128)(2,1)S(1)}, bf16[64,1536]{1,0:T(8,128)(2,1)S(1)}, u32[]{:S(2)}, u32[]{:S(2)}) collective-permute-start(bf16[64,1536]{1,0:T(8,128)(2,1)S(1)} %broadcast_select_fusion.11), channel_id=1, source_target_pairs={{0,64},{128,192},{256,320},{384,448},{1,65},{129,193},{257,321},{3... | collective-permute-start | bytes 589832 | tf_op jit(solution)/shard_map/cond/branch_2_fun/ppermute | solution.py:33
  61.3 14.5 %all-to-all-start.1 = ((f32[16,40,256]{2,1,0:T(8,128)}), f32[16,40,256]{2,1,0:T(8,128)S(1)}, u32[]{:S(2)}, u32[]{:S(2)}) async-start(f32[16,40,256]{2,1,0:T(8,128)} %broadcast_in_dim.24), calls=%async_computation.1 | async-start | bytes 1310720 | tf_op jit(solution)/shard_map/all_to_all | solution.py:195
  80.6 28.4 %collective-permute-start.29 = (f32[64,256]{1,0:T(8,128)S(1)}, f32[64,256]{1,0:T(8,128)S(1)}, u32[]{:S(2)}, u32[]{:S(2)}) collective-permute-start(f32[64,256]{1,0:T(8,128)S(1)} %fusion.3), channel_id=1, source_target_pairs={{0,256},{64,320},{128,384},{192,448},{256,0},{320,64},{384,128},{4... | collective-permute-start | bytes 196616 | tf_op jit(solution)/shard_map/ppermute | solution.py:153
  109.0 6.3 %collective-permute-start.30 = (f32[64,256]{1,0:T(8,128)S(1)}, f32[64,256]{1,0:T(8,128)S(1)}, u32[]{:S(2)}, u32[]{:S(2)}) collective-permute-start(f32[64,256]{1,0:T(8,128)S(1)} %broadcast_select_fusion.21), channel_id=1, source_target_pairs={{0,128},{64,192},{128,0},{192,64},{256,384},{320,448},{384,256},{4... | collective-permute-start | bytes 196616 | tf_op jit(solution)/shard_map/ppermute | solution.py:153
  114.1 10.1 %copy-start.1 = (f32[512,128]{1,0:T(8,128)S(1)}, f32[512,128]{1,0:T(8,128)}, u32[]{:S(2)}) copy-start(f32[512,128]{1,0:T(8,128)} %param.9) | copy-start | bytes 786436

commit v3 on v2

--- a/solution.py
+++ b/solution.py
@@ -179,7 +179,8 @@
     offset = panel_start & (rows_dev - 1)
     mine = lax.dynamic_slice_in_dim(signatures, offset + HALF * core, HALF, 0)
     other = lax.dynamic_slice_in_dim(signatures, offset + HALF * (1 - core), HALF, 0)
-    half = jnp.where(core == (owner & 1), mine, lax.ppermute(other, "core", SWAP))
+    swapped = lax.all_gather(other, "core")
+    half = jnp.where(core == (owner & 1), mine, jnp.where(core == 0, swapped[1], swapped[0]))
     low, high = lax.switch(owner >> 1, [panel_tree(i) for i in range(4)], half[: HALF // 2], half[HALF // 2 :])
     parts = call(
         gram_kernel,

time: 126 us -> 124 us (0.984)
  waiting for transfers between devices: 15.5 us -> 10.2 us
  blocking collectives: 49.4 us -> 53.5 us
    ppermute x2, starting transfers between devices: 24.2 us -> 35.4 us  [cross(): moved = lax.ppermute(block, 'zl', [(i, i ^ step) for i in range(8)])]
    all_gather x0 -> x1, blocking collectives: none -> 8.87 us  [local(): swapped = lax.all_gather(other, 'core')]
    ppermute x1 -> x0, starting transfers between devices: 8.79 us -> none  [local(): half = jnp.where(core == owner & 1, mine, lax.ppermute(other, 'core', SWAP))]
    ppermute x2, waiting for transfers between devices: 3.96 us -> 0.01 us  [branch(): moved = lax.ppermute(piece, 'zl', last)]
    all_gather x1, blocking collectives: 8.41 us -> 6.55 us  [window_and_inverse(): lax.all_gather(mid, ROW, axis_index_groups=[[i, i + 1, i + 2, i + 3] for...]
    all_gather x2, blocking collectives: 5.68 us -> 4.18 us  [branch(): out.append(lax.all_gather(piece, 'core'))]
    ppermute x1 -> x0, waiting for transfers between devices: 1.31 us -> none  [local(): half = jnp.where(core == owner & 1, mine, lax.ppermute(other, 'core', SWAP))]
  transfers between devices with their start and end apart: 10 -> 9, of which waited for: 5 -> 1; matrix products, arithmetic and copies ran while one was open for 1% -> 1% of each run, Pallas kernels for 7% -> 7%
where the time goes in v3:
time: 124 us
  blocking collectives  53.5 us (43%)
  starting transfers between devices  43 us (35%)
  waiting for transfers between devices  10.2 us (8%)
  Pallas kernels  9.65 us (8%)
  local copies, waits for them, and re-layouts  2.66 us (2%)
  between operations  2.33 us (2%)
  matrix products  2.3 us (2%)
    ppermute x2, starting transfers between devices, cross(): moved = lax.ppermute(block, 'zl', [(i, i ^ step) for i in range(8)])  35.4 us
    all_to_all x1, blocking collectives, local(): parts = lax.all_to_all(parts, PLANE, 0, 0, tiled=True)  15.3 us
    all_gather x1, blocking collectives, local(): piece = jnp.sum(lax.all_gather(jnp.sum(parts, axis=0), 'zh'), axis=0)  13.9 us
    all_to_all x1, waiting for transfers between devices, local(): lax.all_to_all(jnp.broadcast_to(piece[None], parts.shape), PLANE, 0, 0, t...  10.2 us
    pallas_call x5, Pallas kernels, call(): pl.pallas_call(kernel, out_shape=outs, in_specs=[vmem] * len(args), out_s...  9.65 us
    all_gather x1, blocking collectives, local(): swapped = lax.all_gather(other, 'core')  8.87 us
    all_gather x1, blocking collectives, window_and_inverse(): lax.all_gather(mid, ROW, axis_index_groups=[[i, i + 1, i + 2, i + 3] for...  6.55 us
    all_gather x1, blocking collectives, window_and_inverse(): both = lax.all_gather(jnp.concatenate([diag_half, other]), 'core')  4.73 us
  transfers between devices with their start and end apart: 9, of which 1 were waited for; matrix products, arithmetic and copies ran while one was open for 1% of the time, Pallas kernels for 7%

profile of v3, /device:TPU:1, one launch (start us, length us, event | category | flops | bytes accessed | tf_op | source)
XLA Modules:
  0.0 124.4 jit_solution(11242236261868745841)
XLA Ops:
  1.4 1.0 constant_dynamic-slice_fusion.1
  2.4 8.9 %all-gather.8 = bf16[256,1536]{1,0:T(8,128)(2,1)S(1)} all-gather(bf16[128,1536]{1,0:T(8,128)(2,1)S(1)} %constant_dynamic-slice_fusion.1), channel_id=10, replica_groups=mesh['zl'=8,'core'=2,'y'=4,'x'=4,'zh'=2] {'core'}, dimensions={0}, use_global_device_ids=true | all-gather | bytes 1179648 | tf_op jit(solution)/shard_map/all_gather | solution.py:182
  11.3 0.1 fusion
  11.5 8.6 %conditional.1 = (bf16[2,64,1536]{2,1,0:T(8,128)(2,1)S(1)}, bf16[2,64,1536]{2,1,0:T(8,128)(2,1)S(1)}) conditional(s32[]{:T(128)} %clamp.3, (bf16[64,1536]{1,0:T(8,128)(2,1)S(1)}, bf16[64,1536]{1,0:T(8,128)(2,1)S(1)}) %tuple.24, (bf16[64,1536]{1,0:T(8,128)(2,1)S(1)}, bf16[64,1536]{1,0:T(8,128)(2,1)S(1)}) %tuple.24, ...), branch_computations={%region_0.1_spmd, %region_1.2_spmd, %region_2.3_spmd, %region_3.4_... | conditional | flops 786441 | bytes 11403700 | solution.py:184
  11.5 0.7 collective-permute-start.25
  12.2 0.7 collective-permute-start.22
  12.9 0.0 collective-permute-done.25
  13.0 0.7 collective-permute-start.26
  13.7 0.7 collective-permute-start.23
  14.4 0.7 collective-permute-start.27
  15.1 0.7 collective-permute-start.24
  15.9 2.1 %all-gather.7 = bf16[128,1536]{1,0:T(8,128)(2,1)S(1)} all-gather(bf16[64,1536]{1,0:T(8,128)(2,1)S(1)} %broadcast_select_fusion.18), channel_id=9, replica_groups=mesh['zl'=8,'core'=2,'y'=4,'x'=4,'zh'=2] {'core'}, dimensions={0}, use_global_device_ids=true | all-gather | bytes 589824 | tf_op jit(solution)/shard_map/cond/branch_3_fun/all_gather | solution.py:35
  18.0 2.1 %all-gather.6 = bf16[128,1536]{1,0:T(8,128)(2,1)S(1)} all-gather(bf16[64,1536]{1,0:T(8,128)(2,1)S(1)} %broadcast_select_fusion.19), channel_id=8, replica_groups=mesh['zl'=8,'core'=2,'y'=4,'x'=4,'zh'=2] {'core'}, dimensions={0}, use_global_device_ids=true | all-gather | bytes 589824 | tf_op jit(solution)/shard_map/cond/branch_3_fun/all_gather | solution.py:35
  20.1 0.8 shard_map.59
  20.9 15.3 %all_to_all.10 = f32[16,40,256]{2,1,0:T(8,128)S(1)} all-to-all(f32[16,40,256]{2,1,0:T(8,128)S(1)} %shard_map.59), channel_id=1, replica_groups=mesh['zl'=8,'core'=2,'y'=4,'x'=4,'zh'=2] {'y','x'}, dimensions={0} | all-to-all | bytes 1310720 | tf_op jit(solution)/shard_map/all_to_all | solution.py:194
  36.2 13.9 %all-gather.9 = f32[80,256]{1,0:T(8,128)S(1)} all-gather(f32[40,256]{1,0:T(8,128)S(1)} %reduce_sum.18), channel_id=11, replica_groups=mesh['zl'=8,'core'=2,'y'=4,'x'=4,'zh'=2] {'zh'}, dimensions={0}, use_global_device_ids=true | all-gather | bytes 122880 | tf_op jit(solution)/shard_map/all_gather | solution.py:195
  50.1 0.9 broadcast_in_dim.24
  51.0 3.6 %all-to-all-start.1 = ((f32[16,40,256]{2,1,0:T(8,128)}), f32[16,40,256]{2,1,0:T(8,128)S(1)}, u32[]{:S(2)}, u32[]{:S(2)}) async-start(f32[16,40,256]{2,1,0:T(8,128)} %broadcast_in_dim.24), calls=%async_computation.1 | async-start | bytes 1310720 | tf_op jit(solution)/shard_map/all_to_all | solution.py:196
  55.3 10.2 %all-to-all-done.1 = f32[16,40,256]{2,1,0:T(8,128)S(1)} async-done(((f32[16,40,256]{2,1,0:T(8,128)}), f32[16,40,256]{2,1,0:T(8,128)S(1)}, u32[]{:S(2)}, u32[]{:S(2)}) %all-to-all-start.1) | async-done | bytes 655392 | tf_op jit(solution)/shard_map/all_to_all | solution.py:196
  65.6 4.7 %all-gather.10 = f32[384,256]{1,0:T(8,128)S(1)} all-gather(f32[192,256]{1,0:T(8,128)S(1)} %pad_maximum_fusion), channel_id=12, replica_groups=mesh['zl'=8,'core'=2,'y'=4,'x'=4,'zh'=2] {'core'}, dimensions={0}, use_global_device_ids=true | all-gather | bytes 589824 | tf_op jit(solution)/shard_map/all_gather | solution.py:157
  70.3 27.6 %collective-permute-start.28 = (f32[64,256]{1,0:T(8,128)S(1)}, f32[64,256]{1,0:T(8,128)S(1)}, u32[]{:S(2)}, u32[]{:S(2)}) collective-permute-start(f32[64,256]{1,0:T(8,128)S(1)} %fusion.4), channel_id=1, source_target_pairs={{0,256},{64,320},{128,384},{192,448},{256,0},{320,64},{384,128},{4... | collective-permute-start | bytes 196616 | tf_op jit(solution)/shard_map/ppermute | solution.py:153
  98.0 1.8 %shard_map.60 = (f32[128,128]{1,0:T(8,128)S(1)}, f32[128,128]{1,0:T(8,128)S(1)}, f32[128,128]{1,0:T(8,128)S(1)}) custom-call(f32[128,128]{1,0:T(8,128)S(1)} %get-tuple-element.56.d_ref, f32[8,128]{1,0:T(8,128)S(1)} %slice.95.after_ref), custom_call_target="tpu_custom_call" | custom-call | flops 1000000000 | bytes 1000000 | tf_op jit(solution)/shard_map/pallas_call | solution.py:48
  99.8 0.1 bitcast_add_fusion
  100.0 2.6 %shard_map.61 = (f32[128,128]{1,0:T(8,128)S(1)}, f32[128,128]{1,0:T(8,128)S(1)}, f32[128,128]{1,0:T(8,128)S(1)}) custom-call(f32[128,128]{1,0:T(8,128)S(1)} %get-tuple-element.40.a_ref, f32[128,128]{1,0:T(8,128)S(1)} %get-tuple-element.41.e_ref, f32[128,128]{1,0:T(8,128)S(1)} %get-tuple-element.42.m_in, f32[128,128]{1,0:T(8,128)S(1)} %get-tuple-element.55.d10_ref, ...), custom_call_target="tpu_custom_call" | custom-call | flops 1000000000 | bytes 1000000 | tf_op jit(solution)/shard_map/pallas_call | solution.py:48
  102.6 1.8 %shard_map.62 = (f32[128,128]{1,0:T(8,128)S(1)}, f32[128,128]{1,0:T(8,128)S(1)}, f32[128,128]{1,0:T(8,128)S(1)}) custom-call(f32[128,128]{1,0:T(8,128)S(1)} %get-tuple-element.43.d_ref, f32[8,128]{1,0:T(8,128)S(1)} %slice.95.after_ref), custom_call_target="tpu_custom_call" | custom-call | flops 1000000000 | bytes 1000000 | tf_op jit(solution)/shard_map/pallas_call | solution.py:48
  104.4 7.8 %collective-permute-start.29 = (f32[64,256]{1,0:T(8,128)S(1)}, f32[64,256]{1,0:T(8,128)S(1)}, u32[]{:S(2)}, u32[]{:S(2)}) collective-permute-start(f32[64,256]{1,0:T(8,128)S(1)} %broadcast_select_fusion.21), channel_id=1, source_target_pairs={{0,128},{64,192},{128,0},{192,64},{256,384},{320,448},{384,256},{4... | collective-permute-start | bytes 196616 | tf_op jit(solution)/shard_map/ppermute | solution.py:153
  112.3 2.7 %shard_map.63 = (f32[256,256]{1,0:T(8,128)S(1)}, f32[128,128]{1,0:T(8,128)}) custom-call(f32[128,128]{1,0:T(8,128)S(1)} %get-tuple-element.44.a_ref, f32[128,128]{1,0:T(8,128)S(1)} %get-tuple-element.45.e_ref, f32[128,128]{1,0:T(8,128)S(1)} %get-tuple-element.46.m_in, f32[128,128]{1,0:T(8,128)S(1)} %get-tuple-element.47.m00_ref, ...), custom_call_target="tpu_custom_call" | custom-call | flops 1000000000 | bytes 1000000 | tf_op jit(solution)/shard_map/pallas_call | solution.py:48
  114.9 0.6 convolution_select_fusion
  115.6 0.6 constant_dynamic-slice_fusion
  116.2 6.6 %all-gather.11 = f32[256,256]{1,0:T(8,128)S(1)} all-gather(f32[64,256]{1,0:T(8,128)S(1)} %broadcast_select_fusion.20), channel_id=13, replica_groups={{0,32,64,96},{128,160,192,224},{256,288,320,352},{384,416,448,480},{1,3..., dimensions={0}, use_global_device_ids=true | all-gather | bytes 327680 | tf_op jit(solution)/shard_map/all_gather | solution.py:167
  122.7 0.4 convolution_select_fusion.1
  123.2 1.3 %convolution_subtract_fusion = f32[512,128]{1,0:T(8,128)} fusion(f32[512,128]{1,0:T(8,128)S(1)} %copy-done.1, f32[512,256]{1,0:T(8,128)S(1)} %convolution_select_fusion, f32[128,256]{1,0:T(8,128)S(1)} %convolution_select_fusion.1), kind=kOutput, calls=%fused_computation.25 | convolution fusion | flops 201392128 | bytes 1179648 | tf_op jit(solution)/shard_map/dot_general | solution.py:42
  (35 shorter events, 0.5 us)
Async XLA Ops:
  0.6 10.7 %copy-start = (bf16[512,1536]{1,0:T(8,128)(2,1)S(1)}, bf16[512,1536]{1,0:T(8,128)(2,1)}, u32[]{:S(2)}) copy-start(bf16[512,1536]{1,0:T(8,128)(2,1)} %s_ref.1) | copy-start | bytes 4718596
  11.5 1.4 %collective-permute-start.25 = (bf16[64,1536]{1,0:T(8,128)(2,1)S(1)}, bf16[64,1536]{1,0:T(8,128)(2,1)S(1)}, u32[]{:S(2)}, u32[]{:S(2)}) collective-permute-start(bf16[64,1536]{1,0:T(8,128)(2,1)S(1)} %get-tuple-element.23), channel_id=1, source_target_pairs={{192,448},{193,449},{194,450},{195,451},{196,452},{197,453},{198,4... | collective-permute-start | bytes 589832 | tf_op jit(solution)/shard_map/cond/branch_3_fun/ppermute | solution.py:26
  12.2 1.4 %collective-permute-start.22 = (bf16[64,1536]{1,0:T(8,128)(2,1)S(1)}, bf16[64,1536]{1,0:T(8,128)(2,1)S(1)}, u32[]{:S(2)}, u32[]{:S(2)}) collective-permute-start(bf16[64,1536]{1,0:T(8,128)(2,1)S(1)} %get-tuple-element.22), channel_id=1, source_target_pairs={{192,448},{193,449},{194,450},{195,451},{196,452},{197,453},{198,4... | collective-permute-start | bytes 589832 | tf_op jit(solution)/shard_map/cond/branch_3_fun/ppermute | solution.py:26
  13.0 1.4 %collective-permute-start.26 = (bf16[64,1536]{1,0:T(8,128)(2,1)S(1)}, bf16[64,1536]{1,0:T(8,128)(2,1)S(1)}, u32[]{:S(2)}, u32[]{:S(2)}) collective-permute-start(bf16[64,1536]{1,0:T(8,128)(2,1)S(1)} %broadcast_select_fusion.14), channel_id=1, source_target_pairs={{448,320},{449,321},{450,322},{451,323},{452,324},{453,325},{454,3... | collective-permute-start | bytes 589832 | tf_op jit(solution)/shard_map/cond/branch_3_fun/ppermute | solution.py:28
  13.7 1.4 %collective-permute-start.23 = (bf16[64,1536]{1,0:T(8,128)(2,1)S(1)}, bf16[64,1536]{1,0:T(8,128)(2,1)S(1)}, u32[]{:S(2)}, u32[]{:S(2)}) collective-permute-start(bf16[64,1536]{1,0:T(8,128)(2,1)S(1)} %broadcast_select_fusion.15), channel_id=1, source_target_pairs={{448,320},{449,321},{450,322},{451,323},{452,324},{453,325},{454,3... | collective-permute-start | bytes 589832 | tf_op jit(solution)/shard_map/cond/branch_3_fun/ppermute | solution.py:28
  14.4 1.4 %collective-permute-start.27 = (bf16[64,1536]{1,0:T(8,128)(2,1)S(1)}, bf16[64,1536]{1,0:T(8,128)(2,1)S(1)}, u32[]{:S(2)}, u32[]{:S(2)}) collective-permute-start(bf16[64,1536]{1,0:T(8,128)(2,1)S(1)} %broadcast_select_fusion.16), channel_id=1, source_target_pairs={{64,128},{192,256},{320,384},{65,129},{193,257},{321,385},{66,130}... | collective-permute-start | bytes 589832 | tf_op jit(solution)/shard_map/cond/branch_3_fun/ppermute | solution.py:33
  15.1 2.8 %collective-permute-start.24 = (bf16[64,1536]{1,0:T(8,128)(2,1)S(1)}, bf16[64,1536]{1,0:T(8,128)(2,1)S(1)}, u32[]{:S(2)}, u32[]{:S(2)}) collective-permute-start(bf16[64,1536]{1,0:T(8,128)(2,1)S(1)} %broadcast_select_fusion.17), channel_id=1, source_target_pairs={{64,128},{192,256},{320,384},{65,129},{193,257},{321,385},{66,130}... | collective-permute-start | bytes 589832 | tf_op jit(solution)/shard_map/cond/branch_3_fun/ppermute | solution.py:33
  51.0 14.5 %all-to-all-start.1 = ((f32[16,40,256]{2,1,0:T(8,128)}), f32[16,40,256]{2,1,0:T(8,128)S(1)}, u32[]{:S(2)}, u32[]{:S(2)}) async-start(f32[16,40,256]{2,1,0:T(8,128)} %broadcast_in_dim.24), calls=%async_computation.1 | async-start | bytes 1310720 | tf_op jit(solution)/shard_map/all_to_all | solution.py:196
  70.3 34.1 %collective-permute-start.28 = (f32[64,256]{1,0:T(8,128)S(1)}, f32[64,256]{1,0:T(8,128)S(1)}, u32[]{:S(2)}, u32[]{:S(2)}) collective-permute-start(f32[64,256]{1,0:T(8,128)S(1)} %fusion.4), channel_id=1, source_target_pairs={{0,256},{64,320},{128,384},{192,448},{256,0},{320,64},{384,128},{4... | collective-permute-start | bytes 196616 | tf_op jit(solution)/shard_map/ppermute | solution.py:153
  104.4 11.7 %collective-permute-start.29 = (f32[64,256]{1,0:T(8,128)S(1)}, f32[64,256]{1,0:T(8,128)S(1)}, u32[]{:S(2)}, u32[]{:S(2)}) collective-permute-start(f32[64,256]{1,0:T(8,128)S(1)} %broadcast_select_fusion.21), channel_id=1, source_target_pairs={{0,128},{64,192},{128,0},{192,64},{256,384},{320,448},{384,256},{4... | collective-permute-start | bytes 196616 | tf_op jit(solution)/shard_map/ppermute | solution.py:153
  114.9 8.2 %copy-start.1 = (f32[512,128]{1,0:T(8,128)S(1)}, f32[512,128]{1,0:T(8,128)}, u32[]{:S(2)}) copy-start(f32[512,128]{1,0:T(8,128)} %param.9) | copy-start | bytes 786436

commit v4 on v3

--- a/solution.py
+++ b/solution.py
@@ -207,8 +207,8 @@
     col_ids = panel_start + lax.broadcasted_iota(jnp.int32, gram.shape, 1)
     gram = gram + jnp.where(row_ids == col_ids, ridge[0], 0.0)
     factor = jnp.where(row_ids >= panel_start, mm(gram, inverse, 1, 1), 0.0)
-    window = jnp.where(row >= owner, mm(cut, inverse, 1, 1), 0.0)
-    updated = trailing - mm(factor, window, 1, 1)
+    solved = mm(factor, inverse, 1, 0)
+    updated = trailing - mm(solved, jnp.where(row >= owner, cut, 0.0), 1, 1)
     return lax.dynamic_slice_in_dim(factor, col * 16, 16, 0), updated
 
 

time: 124 us -> 124 us (level)
  transfers between devices with their start and end apart: 9 -> 9, of which waited for: 1 -> 1; matrix products, arithmetic and copies ran while one was open for 1% -> 2% of each run, Pallas kernels for 7% -> 7%
where the time goes in v4:
time: 124 us; the launch traced here: 125 us
  blocking collectives  53.5 us (43%)
  starting transfers between devices  43 us (35%)
  waiting for transfers between devices  10.2 us (8%)
  Pallas kernels  9.65 us (8%)
  local copies, waits for them, and re-layouts  2.66 us (2%)
  matrix products  2.48 us (2%)
  between operations  2.32 us (2%)
    ppermute x2, starting transfers between devices, cross(): moved = lax.ppermute(block, 'zl', [(i, i ^ step) for i in range(8)])  35.4 us
    all_to_all x1, blocking collectives, local(): parts = lax.all_to_all(parts, PLANE, 0, 0, tiled=True)  15.3 us
    all_gather x1, blocking collectives, local(): piece = jnp.sum(lax.all_gather(jnp.sum(parts, axis=0), 'zh'), axis=0)  13.9 us
    all_to_all x1, waiting for transfers between devices, local(): lax.all_to_all(jnp.broadcast_to(piece[None], parts.shape), PLANE, 0, 0, t...  10.2 us
    pallas_call x5, Pallas kernels, call(): pl.pallas_call(kernel, out_shape=outs, in_specs=[vmem] * len(args), out_s...  9.65 us
    all_gather x1, blocking collectives, local(): swapped = lax.all_gather(other, 'core')  8.87 us
    all_gather x1, blocking collectives, window_and_inverse(): lax.all_gather(mid, ROW, axis_index_groups=[[i, i + 1, i + 2, i + 3] for...  6.55 us
    all_gather x1, blocking collectives, window_and_inverse(): both = lax.all_gather(jnp.concatenate([diag_half, other]), 'core')  4.73 us
  transfers between devices with their start and end apart: 9, of which 1 were waited for; matrix products, arithmetic and copies ran while one was open for 2% of the time, Pallas kernels for 7%

profile of v4, /device:TPU:1, one launch (start us, length us, event | category | flops | bytes accessed | tf_op | source)
XLA Modules:
  0.0 124.6 jit_solution(161262918960119868)
XLA Ops:
  1.4 1.0 constant_dynamic-slice_fusion.1
  2.4 8.9 %all-gather.8 = bf16[256,1536]{1,0:T(8,128)(2,1)S(1)} all-gather(bf16[128,1536]{1,0:T(8,128)(2,1)S(1)} %constant_dynamic-slice_fusion.1), channel_id=10, replica_groups=mesh['zl'=8,'core'=2,'y'=4,'x'=4,'zh'=2] {'core'}, dimensions={0}, use_global_device_ids=true | all-gather | bytes 1179648 | tf_op jit(solution)/shard_map/all_gather | solution.py:182
  11.3 0.1 fusion
  11.5 8.6 %conditional.1 = (bf16[2,64,1536]{2,1,0:T(8,128)(2,1)S(1)}, bf16[2,64,1536]{2,1,0:T(8,128)(2,1)S(1)}) conditional(s32[]{:T(128)} %clamp.3, (bf16[64,1536]{1,0:T(8,128)(2,1)S(1)}, bf16[64,1536]{1,0:T(8,128)(2,1)S(1)}) %tuple.24, (bf16[64,1536]{1,0:T(8,128)(2,1)S(1)}, bf16[64,1536]{1,0:T(8,128)(2,1)S(1)}) %tuple.24, ...), branch_computations={%region_0.1_spmd, %region_1.2_spmd, %region_2.3_spmd, %region_3.4_... | conditional | flops 786441 | bytes 11403700 | solution.py:184
  11.5 0.7 collective-permute-start.25
  12.2 0.7 collective-permute-start.22
  13.0 0.7 collective-permute-start.26
  13.6 0.0 collective-permute-done.22
  13.7 0.7 collective-permute-start.23
  14.4 0.7 collective-permute-start.27
  15.1 0.7 collective-permute-start.24
  15.9 2.1 %all-gather.7 = bf16[128,1536]{1,0:T(8,128)(2,1)S(1)} all-gather(bf16[64,1536]{1,0:T(8,128)(2,1)S(1)} %broadcast_select_fusion.18), channel_id=9, replica_groups=mesh['zl'=8,'core'=2,'y'=4,'x'=4,'zh'=2] {'core'}, dimensions={0}, use_global_device_ids=true | all-gather | bytes 589824 | tf_op jit(solution)/shard_map/cond/branch_3_fun/all_gather | solution.py:35
  18.0 2.1 %all-gather.6 = bf16[128,1536]{1,0:T(8,128)(2,1)S(1)} all-gather(bf16[64,1536]{1,0:T(8,128)(2,1)S(1)} %broadcast_select_fusion.19), channel_id=8, replica_groups=mesh['zl'=8,'core'=2,'y'=4,'x'=4,'zh'=2] {'core'}, dimensions={0}, use_global_device_ids=true | all-gather | bytes 589824 | tf_op jit(solution)/shard_map/cond/branch_3_fun/all_gather | solution.py:35
  20.1 0.8 shard_map.59
  20.9 15.3 %all_to_all.10 = f32[16,40,256]{2,1,0:T(8,128)S(1)} all-to-all(f32[16,40,256]{2,1,0:T(8,128)S(1)} %shard_map.59), channel_id=1, replica_groups=mesh['zl'=8,'core'=2,'y'=4,'x'=4,'zh'=2] {'y','x'}, dimensions={0} | all-to-all | bytes 1310720 | tf_op jit(solution)/shard_map/all_to_all | solution.py:194
  36.2 13.9 %all-gather.9 = f32[80,256]{1,0:T(8,128)S(1)} all-gather(f32[40,256]{1,0:T(8,128)S(1)} %reduce_sum.18), channel_id=11, replica_groups=mesh['zl'=8,'core'=2,'y'=4,'x'=4,'zh'=2] {'zh'}, dimensions={0}, use_global_device_ids=true | all-gather | bytes 122880 | tf_op jit(solution)/shard_map/all_gather | solution.py:195
  50.1 0.9 broadcast_in_dim.24
  51.0 3.6 %all-to-all-start.1 = ((f32[16,40,256]{2,1,0:T(8,128)}), f32[16,40,256]{2,1,0:T(8,128)S(1)}, u32[]{:S(2)}, u32[]{:S(2)}) async-start(f32[16,40,256]{2,1,0:T(8,128)} %broadcast_in_dim.24), calls=%async_computation.1 | async-start | bytes 1310720 | tf_op jit(solution)/shard_map/all_to_all | solution.py:196
  55.3 10.2 %all-to-all-done.1 = f32[16,40,256]{2,1,0:T(8,128)S(1)} async-done(((f32[16,40,256]{2,1,0:T(8,128)}), f32[16,40,256]{2,1,0:T(8,128)S(1)}, u32[]{:S(2)}, u32[]{:S(2)}) %all-to-all-start.1) | async-done | bytes 655392 | tf_op jit(solution)/shard_map/all_to_all | solution.py:196
  65.6 4.7 %all-gather.10 = f32[384,256]{1,0:T(8,128)S(1)} all-gather(f32[192,256]{1,0:T(8,128)S(1)} %pad_maximum_fusion), channel_id=12, replica_groups=mesh['zl'=8,'core'=2,'y'=4,'x'=4,'zh'=2] {'core'}, dimensions={0}, use_global_device_ids=true | all-gather | bytes 589824 | tf_op jit(solution)/shard_map/all_gather | solution.py:157
  70.3 27.6 %collective-permute-start.28 = (f32[64,256]{1,0:T(8,128)S(1)}, f32[64,256]{1,0:T(8,128)S(1)}, u32[]{:S(2)}, u32[]{:S(2)}) collective-permute-start(f32[64,256]{1,0:T(8,128)S(1)} %fusion.6), channel_id=1, source_target_pairs={{0,256},{64,320},{128,384},{192,448},{256,0},{320,64},{384,128},{4... | collective-permute-start | bytes 196616 | tf_op jit(solution)/shard_map/ppermute | solution.py:153
  98.0 1.8 %shard_map.60 = (f32[128,128]{1,0:T(8,128)S(1)}, f32[128,128]{1,0:T(8,128)S(1)}, f32[128,128]{1,0:T(8,128)S(1)}) custom-call(f32[128,128]{1,0:T(8,128)S(1)} %get-tuple-element.56.d_ref, f32[8,128]{1,0:T(8,128)S(1)} %slice.95.after_ref), custom_call_target="tpu_custom_call" | custom-call | flops 1000000000 | bytes 1000000 | tf_op jit(solution)/shard_map/pallas_call | solution.py:48
  99.8 0.1 bitcast_add_fusion
  100.0 2.6 %shard_map.61 = (f32[128,128]{1,0:T(8,128)S(1)}, f32[128,128]{1,0:T(8,128)S(1)}, f32[128,128]{1,0:T(8,128)S(1)}) custom-call(f32[128,128]{1,0:T(8,128)S(1)} %get-tuple-element.40.a_ref, f32[128,128]{1,0:T(8,128)S(1)} %get-tuple-element.41.e_ref, f32[128,128]{1,0:T(8,128)S(1)} %get-tuple-element.42.m_in, f32[128,128]{1,0:T(8,128)S(1)} %get-tuple-element.55.d10_ref, ...), custom_call_target="tpu_custom_call" | custom-call | flops 1000000000 | bytes 1000000 | tf_op jit(solution)/shard_map/pallas_call | solution.py:48
  102.6 1.8 %shard_map.62 = (f32[128,128]{1,0:T(8,128)S(1)}, f32[128,128]{1,0:T(8,128)S(1)}, f32[128,128]{1,0:T(8,128)S(1)}) custom-call(f32[128,128]{1,0:T(8,128)S(1)} %get-tuple-element.43.d_ref, f32[8,128]{1,0:T(8,128)S(1)} %slice.95.after_ref), custom_call_target="tpu_custom_call" | custom-call | flops 1000000000 | bytes 1000000 | tf_op jit(solution)/shard_map/pallas_call | solution.py:48
  104.4 7.8 %collective-permute-start.29 = (f32[64,256]{1,0:T(8,128)S(1)}, f32[64,256]{1,0:T(8,128)S(1)}, u32[]{:S(2)}, u32[]{:S(2)}) collective-permute-start(f32[64,256]{1,0:T(8,128)S(1)} %broadcast_select_fusion.21), channel_id=1, source_target_pairs={{0,128},{64,192},{128,0},{192,64},{256,384},{320,448},{384,256},{4... | collective-permute-start | bytes 196616 | tf_op jit(solution)/shard_map/ppermute | solution.py:153
  112.3 2.7 %shard_map.63 = (f32[256,256]{1,0:T(8,128)S(1)}, f32[128,128]{1,0:T(8,128)}) custom-call(f32[128,128]{1,0:T(8,128)S(1)} %get-tuple-element.44.a_ref, f32[128,128]{1,0:T(8,128)S(1)} %get-tuple-element.45.e_ref, f32[128,128]{1,0:T(8,128)S(1)} %get-tuple-element.46.m_in, f32[128,128]{1,0:T(8,128)S(1)} %get-tuple-element.47.m00_ref, ...), custom_call_target="tpu_custom_call" | custom-call | flops 1000000000 | bytes 1000000 | tf_op jit(solution)/shard_map/pallas_call | solution.py:48
  114.9 0.6 convolution_select_fusion
  115.6 0.6 fusion.13
  116.1 0.6 constant_dynamic-slice_fusion
  116.8 6.6 %all-gather.11 = f32[256,256]{1,0:T(8,128)S(1)} all-gather(f32[64,256]{1,0:T(8,128)S(1)} %broadcast_select_fusion.20), channel_id=13, replica_groups={{0,32,64,96},{128,160,192,224},{256,288,320,352},{384,416,448,480},{1,3..., dimensions={0}, use_global_device_ids=true | all-gather | bytes 327680 | tf_op jit(solution)/shard_map/all_gather | solution.py:167
  123.3 1.3 %convolution_subtract_fusion = f32[512,128]{1,0:T(8,128)} fusion(f32[512,128]{1,0:T(8,128)S(1)} %copy-done.1, f32[512,256]{1,0:T(8,128)S(1)} %fusion.13, f32[256,256]{1,0:T(8,128)S(1)} %all-gather.11, pred[]{:T(512)S(6)} %ge.16, pred[]{:T(512)S(6)} %eq.84), kind=kOutput, calls=%fused_computation.25 | convolution fusion | flops 201457664 | bytes 1310722 | tf_op jit(solution)/shard_map/dot_general | solution.py:42
  (35 shorter events, 0.5 us)
Async XLA Ops:
  0.6 10.7 %copy-start = (bf16[512,1536]{1,0:T(8,128)(2,1)S(1)}, bf16[512,1536]{1,0:T(8,128)(2,1)}, u32[]{:S(2)}) copy-start(bf16[512,1536]{1,0:T(8,128)(2,1)} %s_ref.1) | copy-start | bytes 4718596
  11.5 1.4 %collective-permute-start.25 = (bf16[64,1536]{1,0:T(8,128)(2,1)S(1)}, bf16[64,1536]{1,0:T(8,128)(2,1)S(1)}, u32[]{:S(2)}, u32[]{:S(2)}) collective-permute-start(bf16[64,1536]{1,0:T(8,128)(2,1)S(1)} %get-tuple-element.23), channel_id=1, source_target_pairs={{192,448},{193,449},{194,450},{195,451},{196,452},{197,453},{198,4... | collective-permute-start | bytes 589832 | tf_op jit(solution)/shard_map/cond/branch_3_fun/ppermute | solution.py:26
  12.2 1.4 %collective-permute-start.22 = (bf16[64,1536]{1,0:T(8,128)(2,1)S(1)}, bf16[64,1536]{1,0:T(8,128)(2,1)S(1)}, u32[]{:S(2)}, u32[]{:S(2)}) collective-permute-start(bf16[64,1536]{1,0:T(8,128)(2,1)S(1)} %get-tuple-element.22), channel_id=1, source_target_pairs={{192,448},{193,449},{194,450},{195,451},{196,452},{197,453},{198,4... | collective-permute-start | bytes 589832 | tf_op jit(solution)/shard_map/cond/branch_3_fun/ppermute | solution.py:26
  13.0 1.4 %collective-permute-start.26 = (bf16[64,1536]{1,0:T(8,128)(2,1)S(1)}, bf16[64,1536]{1,0:T(8,128)(2,1)S(1)}, u32[]{:S(2)}, u32[]{:S(2)}) collective-permute-start(bf16[64,1536]{1,0:T(8,128)(2,1)S(1)} %broadcast_select_fusion.14), channel_id=1, source_target_pairs={{448,320},{449,321},{450,322},{451,323},{452,324},{453,325},{454,3... | collective-permute-start | bytes 589832 | tf_op jit(solution)/shard_map/cond/branch_3_fun/ppermute | solution.py:28
  13.7 1.4 %collective-permute-start.23 = (bf16[64,1536]{1,0:T(8,128)(2,1)S(1)}, bf16[64,1536]{1,0:T(8,128)(2,1)S(1)}, u32[]{:S(2)}, u32[]{:S(2)}) collective-permute-start(bf16[64,1536]{1,0:T(8,128)(2,1)S(1)} %broadcast_select_fusion.15), channel_id=1, source_target_pairs={{448,320},{449,321},{450,322},{451,323},{452,324},{453,325},{454,3... | collective-permute-start | bytes 589832 | tf_op jit(solution)/shard_map/cond/branch_3_fun/ppermute | solution.py:28
  14.4 1.4 %collective-permute-start.27 = (bf16[64,1536]{1,0:T(8,128)(2,1)S(1)}, bf16[64,1536]{1,0:T(8,128)(2,1)S(1)}, u32[]{:S(2)}, u32[]{:S(2)}) collective-permute-start(bf16[64,1536]{1,0:T(8,128)(2,1)S(1)} %broadcast_select_fusion.16), channel_id=1, source_target_pairs={{64,128},{192,256},{320,384},{65,129},{193,257},{321,385},{66,130}... | collective-permute-start | bytes 589832 | tf_op jit(solution)/shard_map/cond/branch_3_fun/ppermute | solution.py:33
  15.1 2.8 %collective-permute-start.24 = (bf16[64,1536]{1,0:T(8,128)(2,1)S(1)}, bf16[64,1536]{1,0:T(8,128)(2,1)S(1)}, u32[]{:S(2)}, u32[]{:S(2)}) collective-permute-start(bf16[64,1536]{1,0:T(8,128)(2,1)S(1)} %broadcast_select_fusion.17), channel_id=1, source_target_pairs={{64,128},{192,256},{320,384},{65,129},{193,257},{321,385},{66,130}... | collective-permute-start | bytes 589832 | tf_op jit(solution)/shard_map/cond/branch_3_fun/ppermute | solution.py:33
  51.0 14.5 %all-to-all-start.1 = ((f32[16,40,256]{2,1,0:T(8,128)}), f32[16,40,256]{2,1,0:T(8,128)S(1)}, u32[]{:S(2)}, u32[]{:S(2)}) async-start(f32[16,40,256]{2,1,0:T(8,128)} %broadcast_in_dim.24), calls=%async_computation.1 | async-start | bytes 1310720 | tf_op jit(solution)/shard_map/all_to_all | solution.py:196
  70.3 34.1 %collective-permute-start.28 = (f32[64,256]{1,0:T(8,128)S(1)}, f32[64,256]{1,0:T(8,128)S(1)}, u32[]{:S(2)}, u32[]{:S(2)}) collective-permute-start(f32[64,256]{1,0:T(8,128)S(1)} %fusion.6), channel_id=1, source_target_pairs={{0,256},{64,320},{128,384},{192,448},{256,0},{320,64},{384,128},{4... | collective-permute-start | bytes 196616 | tf_op jit(solution)/shard_map/ppermute | solution.py:153
  104.4 12.3 %collective-permute-start.29 = (f32[64,256]{1,0:T(8,128)S(1)}, f32[64,256]{1,0:T(8,128)S(1)}, u32[]{:S(2)}, u32[]{:S(2)}) collective-permute-start(f32[64,256]{1,0:T(8,128)S(1)} %broadcast_select_fusion.21), channel_id=1, source_target_pairs={{0,128},{64,192},{128,0},{192,64},{256,384},{320,448},{384,256},{4... | collective-permute-start | bytes 196616 | tf_op jit(solution)/shard_map/ppermute | solution.py:153
  114.9 8.4 %copy-start.1 = (f32[512,128]{1,0:T(8,128)S(1)}, f32[512,128]{1,0:T(8,128)}, u32[]{:S(2)}) copy-start(f32[512,128]{1,0:T(8,128)} %param.9) | copy-start | bytes 786436
